TPU v7x, 32 devices: a whole 2x2x4 slice. The times are simulated.
32 devices in a mesh: prow: 8 (over z, core), pcol: 4 (over y, x).
Axes of the slice: x: 2, y: 2, z: 4, core: 2. Of those that a mesh axis runs over, the one named last changes fastest.
Arguments:
- root_inverse: float32 [4, 8, 128, 8, 4, 128], P(None, 'prow', None, None, 'pcol'), as said below
- lower_one: float32 [4, 8, 128, 4, 4, 128], P(None, 'prow', None, None, 'pcol'), may hold values from -0.125 to 0.125
- lower_two: float32 [6, 8, 128, 4, 4, 128], P(None, 'prow', None, None, 'pcol'), may hold values from -0.15625 to 0.15625
- dinv_one: float32 [2, 8, 128, 4, 4, 128], P(None, 'prow', None, None, 'pcol'), as said below
- dinv_two: float32 [2, 8, 128, 4, 4, 128], P(None, 'prow', None, None, 'pcol'), as said below
- seg_one: int32 [16], replicated, may hold values from 0 to 2, as said below
- seg_two: int32 [16], replicated, may hold values from 0 to 3, as said below
- parent_two: int32 [4], replicated, may hold values from 0 to 2
- pattern_one: int32 [3, 32], replicated, may hold values 0 or 1
- pattern_two: int32 [4, 48], replicated, may hold values 0 or 1
Outputs:
- inverse_one: float32 [2, 8, 128, 4, 4, 128], P(None, 'prow', None, None, 'pcol')
- inverse_two: float32 [2, 8, 128, 4, 4, 128], P(None, 'prow', None, None, 'pcol')
Inputs may be any that keep to these rules, and one draw needn't show every extreme that they name: `root_inverse`: Block-diagonal over supernodes is not implied; this is a symmetric matrix. `dinv_one`: Symmetric, and zero in every block whose row and column blocks belong to different supernodes of seg_one. `dinv_two`: Symmetric, and zero in every block whose row and column blocks belong to different supernodes of seg_two. `seg_one`: never falls; every supernode 0 to 2 has 1 to 8 consecutive blocks, one exactly 8. `seg_two`: never falls; every supernode 0 to 3 has 1 to 8 consecutive blocks, one exactly 8.
All inputs are finite; a program needn't handle non-finite values.
Results may differ from a plain program's by a relative error of at most 0.00005.
Values sent between devices are 32-bit elements; how exact they have to be, the bound alone decides.
No kernel may reach another device: no remote copies, remote signals or barrier semaphores. Data moves between devices by JAX's collectives and lax.ppermute only.
A program may use at most 128 MiB of HBM per device.

v0:
```python
import jax
import jax.numpy as jnp
from jax import lax
from jax.sharding import PartitionSpec as P

highest = lax.Precision.HIGHEST


def contract(left_side, right_side):
    return lax.dot_general(
        left_side,
        right_side,
        (((0,), (0,)), ((), ())),
        precision=highest,
        preferred_element_type=jnp.float32,
    )


def flatten_local(blocks):
    squeezed = blocks[:, 0, :, :, 0, :]
    return squeezed.reshape(
        squeezed.shape[0] * squeezed.shape[1], squeezed.shape[2] * squeezed.shape[3]
    )


def to_blocks(matrix, block_width):
    return matrix.reshape(
        matrix.shape[0] // block_width,
        1,
        block_width,
        matrix.shape[1] // block_width,
        1,
        block_width,
    )


def apply_mask(matrix, block_mask, block_width):
    row_blocks = block_mask.shape[0]
    col_blocks = block_mask.shape[1]
    shaped = matrix.reshape(row_blocks, block_width, col_blocks, block_width)
    return (shaped * block_mask[:, None, :, None]).reshape(
        row_blocks * block_width, col_blocks * block_width
    )


def split_rows(matrix, pieces, block_width):
    return matrix.reshape(
        matrix.shape[0] // (pieces * block_width), pieces, block_width, matrix.shape[1]
    )


def merge_rows(blocks):
    return blocks.reshape(blocks.shape[0] * blocks.shape[1] * blocks.shape[2], blocks.shape[3])


def row_panel(gathered):
    picked = gathered[:, 0]
    return picked.reshape(
        picked.shape[0] * picked.shape[1], picked.shape[2] * picked.shape[3] * picked.shape[4]
    )


def same_mask(first_ids, second_ids):
    return (first_ids[:, None] == second_ids[None, :]).astype(jnp.float32)


def on_device(
    root_inverse,
    lower_one,
    lower_two,
    dinv_one,
    dinv_two,
    seg_one,
    seg_two,
    parent_two,
    pattern_one,
    pattern_two,
):
    block_width = root_inverse.shape[2]
    prow_total = lax.axis_size("prow")
    pcol_total = lax.axis_size("pcol")
    prow_place = lax.axis_index("prow")
    pcol_place = lax.axis_index("pcol")
    root_blocks = pattern_one.shape[1]
    first_nodes = pattern_one.shape[0]
    second_nodes = pattern_two.shape[0]

    def row_ids(amount):
        return jnp.arange(amount, dtype=jnp.int32) * prow_total + prow_place

    def col_ids(amount):
        return jnp.arange(amount, dtype=jnp.int32) * pcol_total + pcol_place

    root_rows = row_ids(root_inverse.shape[0])
    first_cols = col_ids(lower_one.shape[3])
    seg_cols = seg_one[first_cols]
    pick_first = same_mask(seg_cols, jnp.arange(first_nodes, dtype=jnp.int32))
    mask_one = jnp.dot(pick_first, pattern_one[:, root_rows].astype(jnp.float32)).T
    masked_one = apply_mask(flatten_local(lower_one), mask_one, block_width)
    second_rows = row_ids(lower_two.shape[0])
    second_cols = col_ids(lower_two.shape[3])
    seg_two_cols = seg_two[second_cols]
    parent_cols = parent_two[seg_two_cols]
    pick_second = same_mask(seg_two_cols, jnp.arange(second_nodes, dtype=jnp.int32))
    own_pattern = jnp.dot(pick_second, pattern_two[:, second_rows].astype(jnp.float32))
    pick_parent = same_mask(parent_cols, jnp.arange(first_nodes, dtype=jnp.int32))
    root_reach = jnp.dot(
        pick_parent, pattern_one[:, jnp.minimum(second_rows, root_blocks - 1)].astype(jnp.float32)
    )
    level_index = jnp.clip(second_rows - root_blocks, 0, seg_one.shape[0] - 1)
    level_reach = (seg_one[level_index][None, :] == parent_cols[:, None]).astype(jnp.float32)
    reachable = jnp.where((second_rows < root_blocks)[None, :], root_reach, level_reach)
    mask_two = (own_pattern * reachable).T
    masked_two = apply_mask(flatten_local(lower_two), mask_two, block_width)
    root_local = flatten_local(root_inverse)
    root_gathered, first_gathered, second_gathered = (
        lax.all_gather(root_inverse, "pcol", axis=4, tiled=True),
        lax.all_gather(to_blocks(masked_one, block_width), "pcol", axis=4, tiled=True),
        lax.all_gather(to_blocks(masked_two, block_width), "pcol", axis=4, tiled=True),
    )
    root_full = row_panel(root_gathered)
    first_full = row_panel(first_gathered)
    second_full = row_panel(second_gathered)
    turned_part = split_rows(contract(first_full, root_local), prow_total, block_width)
    solved_part = split_rows(contract(root_full, masked_one), prow_total, block_width)
    solved_blocks, turned_blocks = (
        lax.psum_scatter(solved_part, "prow", scatter_dimension=1, tiled=True),
        lax.psum_scatter(turned_part, "prow", scatter_dimension=1, tiled=True),
    )
    solved_one = merge_rows(solved_blocks)
    turned_one = merge_rows(turned_blocks)
    diag_part = split_rows(contract(first_full, solved_one), prow_total, block_width)
    diag_one = merge_rows(lax.psum_scatter(diag_part, "prow", scatter_dimension=1, tiled=True))
    same_one = same_mask(seg_one[row_ids(dinv_one.shape[0])], seg_one[col_ids(dinv_one.shape[3])])
    inverse_one = apply_mask(flatten_local(dinv_one) + diag_one, same_one, block_width)
    region = jnp.concatenate(
        [
            jnp.concatenate([root_local, -solved_one], axis=1),
            jnp.concatenate([-turned_one, inverse_one], axis=1),
        ],
        axis=0,
    )
    region_gathered = lax.all_gather(to_blocks(region, block_width), "pcol", axis=4, tiled=True)
    product_part = split_rows(
        contract(row_panel(region_gathered), masked_two), prow_total, block_width
    )
    solved_two = merge_rows(lax.psum_scatter(product_part, "prow", scatter_dimension=1, tiled=True))
    diag_two_part = split_rows(contract(second_full, solved_two), prow_total, block_width)
    diag_two = merge_rows(lax.psum_scatter(diag_two_part, "prow", scatter_dimension=1, tiled=True))
    same_two = same_mask(seg_two[row_ids(dinv_two.shape[0])], seg_two[col_ids(dinv_two.shape[3])])
    inverse_two = apply_mask(flatten_local(dinv_two) + diag_two, same_two, block_width)
    return (to_blocks(inverse_one, block_width), to_blocks(inverse_two, block_width))


def solution(mesh):
    return jax.shard_map(
        on_device,
        mesh=mesh,
        in_specs=(
            P(None, "prow", None, None, "pcol", None),
            P(None, "prow", None, None, "pcol", None),
            P(None, "prow", None, None, "pcol", None),
            P(None, "prow", None, None, "pcol", None),
            P(None, "prow", None, None, "pcol", None),
            P(),
            P(),
            P(),
            P(),
            P(),
        ),
        out_specs=(
            P(None, "prow", None, None, "pcol", None),
            P(None, "prow", None, None, "pcol", None),
        ),
        check_vma=False,
    )
```

profile of v0, /device:TPU:4, one launch (start us, length us, event | category | flops | bytes accessed | tf_op | source)
XLA Modules:
  0.0 1183.2 jit_solution(12233576181990154485)
XLA Ops:
  7.2 0.7 all-gather.7.cloned.1.call-update
  8.0 0.8 copy.46
  9.3 0.6 gather_fusion.1
  10.2 2.4 copy_multiply_fusion.1
  12.6 1.9 copy.50
  14.5 84.2 %all-gather.7.cloned.1.call-done = f32[4,1,128,8,4,128]{5,3,2,1,0,4:T(8,128)} async-done(((f32[4,1,128,8,1,128]{5,3,2,1,0,4:T(8,128)}), f32[4,1,128,8,4,128]{5,3,2,1,0,4:T(8,128)}) %all-gather.7.cloned.1.call-update) | async-done | bytes 8388624 | tf_op jit(solution)/shard_map/all_gather | solution.py:117
  98.7 12.3 %copy.52 = f32[4,1,128,8,4,128]{5,4,3,2,0,1:T(4,128)} copy(f32[4,1,128,8,4,128]{5,3,2,1,0,4:T(8,128)} %all-gather.7.cloned.1.call-done) | data formatting | bytes 16777216 | tf_op jit(solution)/shard_map/all_gather | solution.py:117
  111.0 10.7 reshape_squeeze.20
  121.7 15.6 %convolution_bitcast_fusion = f32[64,8,32,128]{3,1,2,0:T(8,128)S(1)} fusion(f32[512,4096]{1,0:T(8,128)} %reshape_squeeze.20, f32[64,8,4,128]{3,2,1,0:T(4,128)S(1)} %bitcast.137), kind=kOutput, calls=%fused_computation.10 | convolution fusion | flops 12884901888 | bytes 17825792 | tf_op jit(solution)/shard_map/dot_general | solution.py:10
  137.3 5.0 copy.79
  142.4 10.1 copy.53
  152.5 1.5 copy-done.4
  154.0 2.1 reshape.320
  156.1 7.0 copy.48
  163.1 5.5 reshape_squeeze.19
  168.6 5.5 copy.49
  174.1 18.1 %fusion = f32[2,8,128,1024]{3,2,1,0:T(8,128)} fusion(f32[2,8,128,512]{3,2,1,0:T(8,128)} %bitcast.128, f32[512,1024,1,1]{1,0,2,3:T(8,128)} %reshape.320), kind=kOutput, calls=%fused_computation.12 | convolution fusion | flops 12884901888 | bytes 14680064 | tf_op jit(solution)/shard_map/dot_general | solution.py:10
  192.3 53.0 %reduce-scatter.14.cloned.1.call-done = f32[4,1,128,512]{3,2,0,1:T(8,128)} async-done(((f32[4,8,128,512]{3,2,0,1:T(8,128)}), f32[4,1,128,512]{3,2,0,1:T(8,128)}) %reduce-scatter.14.cloned.1.call-update) | async-done | bytes 1048592 | tf_op jit(solution)/shard_map/reduce_scatter | solution.py:127
  245.2 10.3 fusion.20
  256.3 1.8 copy.92
  258.8 1.1 bitcast_negate_fusion
  259.8 249.2 %all-reduce.13.cloned.1.call-done = (f32[2,8,128,512]{3,2,1,0:T(8,128)}, f32[2,8,128,1024]{3,2,1,0:T(8,128)}) async-done(((f32[2,8,128,512]{3,2,1,0:T(8,128)}, f32[2,8,128,1024]{3,2,1,0:T(8,128)}), (f32[2,8,128,512]{3,2,1,0:T(8,128)}, f32[2,8,128,1024]{3,2,1,0:T(8,128)})) %all-reduce.13.cloned.1.call-update) | async-done | bytes 12582928
  509.0 1.6 constant_dynamic-slice_fusion.2
  510.7 1.9 dynamic-slice_negate_fusion
  512.7 1.2 bitcast_multiply_fusion
  513.9 2.7 maximum_maximum_fusion
  516.6 6.7 reshape.244
  523.2 6.4 copy.61
  530.4 0.6 gather_fusion.7
  531.0 0.6 gather_fusion.4
  531.8 0.6 gather_fusion.6
  533.5 1.3 copy_multiply_fusion
  534.9 2.4 copy.64
  538.0 168.0 %all-gather.11.cloned.1.call-done = f32[6,1,128,12,4,128]{5,2,3,1,0,4:T(8,128)} async-done(((f32[6,1,128,12,1,128]{5,2,3,1,0,4:T(8,128)}), f32[6,1,128,12,4,128]{5,2,3,1,0,4:T(8,128)}) %all-gather.11.cloned.1.call-update) | async-done | bytes 18874384 | tf_op jit(solution)/shard_map/all_gather | solution.py:143
  706.0 23.8 %copy.62 = f32[6,1,128,12,4,128]{5,4,3,2,0,1:T(4,128)} copy(f32[6,1,128,12,4,128]{5,2,3,1,0,4:T(8,128)} %all-gather.11.cloned.1.call-done) | data formatting | bytes 37748736 | tf_op jit(solution)/shard_map/all_gather | solution.py:143
  729.7 22.0 %reshape_squeeze.24 = f32[768,6144]{1,0:T(8,128)} reshape(f32[6,1,128,12,4,128]{5,4,3,2,0,1:T(4,128)} %copy.62) | data formatting | bytes 37748736 | tf_op jit(solution)/shard_map/reshape;squeeze | solution.py:58
  751.7 18.7 %copy.63 = f32[6144,768]{1,0:T(8,128)} copy(f32[6144,768]{0,1:T(8,128)} %bitcast.126) | data formatting | bytes 37748736 | tf_op jit(solution)/shard_map/dot_general | solution.py:10
  770.4 34.9 %fusion.2 = f32[6,8,128,512]{3,2,1,0:T(8,128)} fusion(f32[6,8,128,768]{3,2,1,0:T(8,128)} %bitcast.127, f32[768,512,1,1]{1,0,2,3:T(8,128)S(1)} %reshape.321), kind=kOutput, calls=%fused_computation.14 | convolution fusion | flops 28991029248 | bytes 33030144 | tf_op jit(solution)/shard_map/dot_general | solution.py:10
  805.6 9.5 copy.59
  815.2 7.9 reshape_squeeze.21
  823.0 6.6 copy.60
  829.7 230.4 %all-reduce.9.cloned.1.call-done = f32[6,8,128,512]{3,2,1,0:T(8,128)} async-done(((f32[6,8,128,512]{3,2,1,0:T(8,128)}), f32[6,8,128,512]{3,2,1,0:T(8,128)}) %all-reduce.9.cloned.1.call-update) | async-done | bytes 12582928
  1060.1 2.1 constant_dynamic-slice_fusion.1
  1062.2 13.6 %fusion.21 = f32[2,8,128,512]{3,2,1,0:T(8,128)} fusion(f32[2,8,128,768]{3,2,1,0:T(8,128)} %bitcast.131, f32[768,512,1,1]{1,0,3,2:T(8,128)S(1)} %bitcast.139), kind=kOutput, calls=%fused_computation.67 | convolution fusion | flops 9663676416 | bytes 12058624 | tf_op jit(solution)/shard_map/dot_general | solution.py:10
  1077.1 1.4 add_multiply_fusion.1
  1078.5 94.1 %all-reduce.11.cloned.1.call-done = f32[2,8,128,512]{3,2,1,0:T(8,128)} async-done(((f32[2,8,128,512]{3,2,1,0:T(8,128)}), f32[2,8,128,512]{3,2,1,0:T(8,128)}) %all-reduce.11.cloned.1.call-update) | async-done | bytes 4194320
  1172.6 1.6 constant_dynamic-slice_fusion
  1174.5 1.4 add_multiply_fusion
  (77 shorter events, 6.9 us)
Async XLA Ops:
  7.2 2.2 copy-start
  7.2 91.5 %all-gather.7.cloned.1.call-start = ((), (), s32[]{:S(2)}) async-start(), calls=%async_computation.2 | async-start | bytes 10485760 | tf_op jit(solution)/shard_map/all_gather | solution.py:117
  7.9 148.2 %all-gather.5.cloned.1.call-start = ((), (), s32[]{:S(2)}) async-start(), calls=%async_computation.1 | async-start | bytes 5242880 | tf_op jit(solution)/shard_map/all_gather | solution.py:118
  12.6 232.6 %reduce-scatter.14.cloned.1.call-start = ((), (), s32[]{:S(2)}) async-start(), calls=%async_computation.3 | async-start | bytes 9437184 | tf_op jit(solution)/shard_map/reduce_scatter | solution.py:127
  152.4 1.6 copy-start.4
  152.5 356.6 %all-reduce.13.cloned.1.call-start = ((), (), s32[]{:S(2)}) async-start(), calls=%async_computation.8 | async-start | bytes 25165824
  255.5 2.6 copy-start.14
  255.5 3.2 copy-start.8
  255.5 450.4 %all-gather.11.cloned.1.call-start = ((), (), s32[]{:S(2)}) async-start(), calls=%async_computation.5 | async-start | bytes 23592960 | tf_op jit(solution)/shard_map/all_gather | solution.py:143
  258.1 255.8 %copy-start.5 = (f32[64,8,8,128]{3,1,2,0:T(8,128)S(1)}, f32[64,8,8,128]{3,1,2,0:T(8,128)}, u32[]{:S(2)}) copy-start(f32[64,8,8,128]{3,1,2,0:T(8,128)} %copy.92) | copy-start | bytes 6291460
  259.8 254.1 %copy-start.9 = (f32[512,512]{1,0:T(8,128)S(1)}, f32[512,512]{1,0:T(8,128)}, u32[]{:S(2)}) copy-start(f32[512,512]{1,0:T(8,128)} %bitcast_negate_fusion) | copy-start | bytes 3145732
  510.7 2.0 copy-start.6
  529.7 1.3 copy-start.2
  529.7 2.0 copy-start.13
  529.7 2.1 copy-start.3
  529.7 3.8 copy-start.11
  529.7 275.9 %all-gather.9.cloned.1.call-start = ((), (), s32[]{:S(2)}) async-start(), calls=%async_computation.4 | async-start | bytes 7864320 | tf_op jit(solution)/shard_map/all_gather | solution.py:119
  534.8 525.2 %all-reduce.9.cloned.1.call-start = ((), (), s32[]{:S(2)}) async-start(), calls=%async_computation.6 | async-start | bytes 25165824
  805.3 367.3 %all-reduce.11.cloned.1.call-start = ((), (), s32[]{:S(2)}) async-start(), calls=%async_computation.7 | async-start | bytes 8388608
  1075.7 1.2 copy-start.7
  1075.8 1.4 copy-start.10
  1075.8 100.1 %copy-start.1 = (s32[16]{0:T(128)S(1)}, s32[16]{0:T(128)}, u32[]{:S(2)}) copy-start(s32[16]{0:T(128)} %param.15) | copy-start | bytes 196
  1075.8 98.7 %copy-start.12 = (f32[2,1,128,4,1,128]{5,4,3,2,1,0:T(1,128)S(1)}, f32[2,1,128,4,1,128]{5,4,3,2,1,0:T(1,128)}, u32[]{:S(2)}) copy-start(f32[2,1,128,4,1,128]{5,4,3,2,1,0:T(1,128)} %param.14) | copy-start | bytes 1572868
Sparse Core Ops, SparseCore 0:
  9.9 88.7 all-gather.6
  100.5 52.6 all-gather.4
  155.6 89.5 reduce-scatter.13
  255.6 253.3 all-reduce.12
  529.8 176.0 all-gather.10
  707.7 70.1 all-gather.8
  805.4 254.6 all-reduce.8
  1075.9 96.6 all-reduce.10
where the time goes:
time: 1190 us; the launch traced here: 1180 us
  waiting for transfers between devices  880 us (74%)
  local copies, waits for them, and re-layouts  181 us (15%)
  matrix products  93.1 us (8%)
  between operations  14.9 us (1%)
  other arithmetic  13.4 us (1%)
    unnamed x11, waiting for transfers between devices  575 us
    all_gather x1, waiting for transfers between devices, on_device(): lax.all_gather(to_blocks(region, block_width), 'pcol', axis=4, tiled=True)  168 us
    dot_general x5, matrix products, contract(): lax.dot_general(left_side, right_side, (((0,), (0,)), ((), ())), precisio...  92.5 us
    all_gather x1, waiting for transfers between devices, on_device(): lax.all_gather(root_inverse, 'pcol', axis=4, tiled=True)  84.2 us
    reduce_scatter x1, waiting for transfers between devices, on_device(): lax.psum_scatter(solved_part, 'prow', scatter_dimension=1, tiled=True)  53 us
    another operation x4, local copies, waits for them, and re-layouts, row_panel(): picked.reshape(picked.shape[0] * picked.shape[1], picked.shape[2] * picke...  46 us
    dot_general x3, local copies, waits for them, and re-layouts, contract(): lax.dot_general(left_side, right_side, (((0,), (0,)), ((), ())), precisio...  30.8 us
  transfers between devices with their start and end apart: 8, of which 6 were waited for; matrix products, arithmetic and copies ran while one was open for 20% of the time, Pallas kernels for 0%

commit v1 on v0

v1 whole, which is shorter than its diff:
```python
import functools

import jax
import jax.numpy as jnp
from jax import lax
from jax.experimental import pallas as pl
from jax.experimental.pallas import tpu as pltpu
from jax.sharding import PartitionSpec as P

VMEM_LIMIT = 56 * 1024 * 1024
F32 = jnp.float32
BOTH = ("prow", "pcol")


def halves(value):
    high = value.astype(jnp.bfloat16)
    low = (value - high.astype(F32)).astype(jnp.bfloat16)
    return high, low


def product(left, right):
    left_high, left_low = left
    right_high, right_low = right
    dot = functools.partial(jnp.dot, preferred_element_type=F32)
    return dot(left_high, right_high) + (dot(left_high, right_low) + dot(left_low, right_high))


def vmem_call(kernel, outs, smem_args, vmem_args, scratch=(), flops=0, after=()):
    def body(*refs):
        kernel(*refs[len(after) :])

    return pl.pallas_call(
        body,
        out_shape=outs,
        in_specs=[pl.BlockSpec(memory_space=pl.ANY)] * len(after)
        + [pl.BlockSpec(memory_space=pltpu.SMEM)] * len(smem_args)
        + [pl.BlockSpec(memory_space=pltpu.VMEM)] * len(vmem_args),
        out_specs=jax.tree.map(lambda _: pl.BlockSpec(memory_space=pltpu.VMEM), outs),
        scratch_shapes=scratch,
        compiler_params=pltpu.CompilerParams(vmem_limit_bytes=VMEM_LIMIT),
        cost_estimate=pl.CostEstimate(
            flops=flops,
            bytes_accessed=sum(4 * arg.size for arg in vmem_args),
            transcendentals=0,
        ),
    )(*after, *smem_args, *vmem_args)


def out_shape(*dims):
    return jax.ShapeDtypeStruct(dims, F32)


class Layout:
    def __init__(self, prow, pcol, width):
        self.prow, self.pcol, self.width = prow, pcol, width
        self.ratio = prow // pcol

    def blocks(self, columns):
        for part in range(self.ratio):
            for group in range(columns // self.ratio):
                yield part * (columns // self.ratio) + group, group * self.ratio + part

    def column_id(self, column, pcol_place):
        return column * self.pcol + pcol_place

    def read(self, ref, row, column, columns):
        return ref[pl.ds(row * self.width * columns + column, self.width, stride=columns), :]

    def lanes(self, index):
        return slice(index * self.width, (index + 1) * self.width)


def first_kernel(lay, counts, place_ref, seg_one, seg_two, parent, one, two, lower_one, lower_two, *outs):
    first_ref, level_ref = outs
    root_count, level_count, one_columns, two_columns, root_total = counts
    prow_place, pcol_place = place_ref[0], place_ref[1]
    for index, column in lay.blocks(one_columns):
        node = seg_one[lay.column_id(column, pcol_place)]
        for row in range(root_count):
            keep = one[node, row * lay.prow + prow_place]
            block = lay.read(lower_one, row, column, one_columns)
            first_ref[lay.lanes(row), lay.lanes(index)] = block * keep.astype(F32)
    for index, column in lay.blocks(two_columns):
        node = seg_two[lay.column_id(column, pcol_place)]
        above = parent[node]
        total = jnp.zeros((lay.width, lay.width), F32)
        for row in range(level_count):
            level_row = row * lay.prow + prow_place
            keep = jnp.where(seg_one[level_row] == above, two[node, root_total + level_row], 0)
            block = lay.read(lower_two, root_count + row, column, two_columns)
            total = total + block * keep.astype(F32)
        level_ref[:, lay.lanes(index)] = total


def root_kernel(lay, root_count, root_columns, root, root_ref):
    for index, column in lay.blocks(root_columns):
        for row in range(root_count):
            block = lay.read(root, row, column, root_columns)
            root_ref[lay.lanes(row), lay.lanes(index)] = block


def second_kernel(lay, counts, place_ref, seg_two, parent, one, two, lower_two, dinv, *refs):
    level_refs = refs[:-3]
    second_ref, dinv_ref, stack_ref = refs[-3:]
    for slot, level_ref in enumerate(level_refs):
        stack_ref[slot] = level_ref[...]
    root_count, level_count, one_columns, two_columns, root_total = counts
    prow_place, pcol_place = place_ref[0], place_ref[1]
    for index, column in lay.blocks(two_columns):
        node = seg_two[lay.column_id(column, pcol_place)]
        above = parent[node]
        for row in range(root_count):
            root_row = row * lay.prow + prow_place
            keep = two[node, root_row] * one[above, root_row]
            block = lay.read(lower_two, row, column, two_columns)
            second_ref[lay.lanes(row), lay.lanes(index)] = block * keep.astype(F32)
    for row in range(level_count):
        for part in range(lay.ratio):
            total = jnp.zeros((lay.width, lay.width), F32)
            for group in range(one_columns // lay.ratio):
                total = total + lay.read(dinv, row, group * lay.ratio + part, one_columns)
            dinv_ref[:, lay.lanes(row * lay.ratio + part)] = total


def fill_panel(piece_refs, panel_ref):
    start = 0
    rows = panel_ref.shape[1]
    for piece_ref in piece_refs:
        place, first = divmod(start, rows)
        panel_ref[place, first : first + piece_ref.shape[0], :] = piece_ref[...]
        start += piece_ref.shape[0]


def panel_columns(lay, panel_ref, rows, source, flip, width):
    place = lax.rem(source, lay.pcol) ^ flip
    start = pl.multiple_of(lax.div(source, lay.pcol) * width, width)
    return panel_ref[place, rows, pl.ds(start, width)]


def gathered_source(lay, place_ref, slot):
    chips = lay.prow // 2
    row = place_ref[0] ^ (slot // chips)
    return lax.rem(row - 2 * (slot % chips) + lay.prow, lay.prow)


def paired_source(lay, place_ref, slot):
    kinds = len(PAIR_FLOWS) + 1
    row = place_ref[0] ^ (slot // kinds)
    kind = slot % kinds
    if kind == 0:
        return row
    plane = lax.div(row, 2)
    source = jnp.int32(0)
    for origin, target in PAIR_FLOWS[kind - 1]:
        source = jnp.where(plane == target, origin, source)
    return source * 2 + lax.rem(row, 2)


def solve_rows(lay, weights, source_of, place_ref, root_ref, slot_refs):
    width = slot_refs[0].shape[0]
    totals = {}
    for slot, slot_ref in enumerate(slot_refs):
        source = source_of(lay, place_ref, slot)
        root_part = panel_columns(lay, root_ref, slice(None), source, 0, width)
        part = product(halves(root_part), halves(slot_ref[...]))
        weight = weights[slot]
        totals[weight] = totals[weight] + part if weight in totals else part
    total = sum(part if weight == 1.0 else part * weight for weight, part in totals.items())
    return total.T


def packed_diagonal(lay, place_ref, segment_ref, left, panel_ref, out_ref, groups, paired):
    rows = out_ref.shape[1]
    depth = left[0].shape[1]
    pcol_place, flip = place_ref[1], place_ref[2]
    for place in range(lay.prow):
        start = (place // lay.pcol) * groups * lay.width
        columns = panel_ref[(place % lay.pcol) ^ flip, :depth, start : start + groups * lay.width]
        result = product(left, halves(columns))
        for index, column in lay.blocks(rows // lay.width):
            node = segment_ref[lay.column_id(column, pcol_place)]
            kept = jnp.zeros((lay.width, lay.width), F32)
            for group in range(groups):
                part = result[lay.lanes(index), lay.lanes(group)]
                same = segment_ref[group * lay.prow + place] == node
                kept = kept + jnp.where(same, part, 0.0)
            target = index
            if paired and place >= lay.pcol:
                target = (index + groups) % (2 * groups)
            out_ref[place, lay.lanes(target), :] = kept


def level_one_kernel(lay, weights, source_of, groups, pieces, place_ref, segment_ref, root_ref, *refs):
    piece_refs, slot_refs = refs[:pieces], refs[pieces:-2]
    out_ref, panel_ref = refs[-2:]
    fill_panel(piece_refs, panel_ref)
    solved = solve_rows(lay, weights, source_of, place_ref, root_ref, slot_refs)
    paired = source_of is paired_source
    packed_diagonal(lay, place_ref, segment_ref, halves(solved), panel_ref, out_ref, groups, paired)


def solve_two_kernel(lay, weights, source_of, place_ref, root_ref, *refs):
    refs[-1][...] = solve_rows(lay, weights, source_of, place_ref, root_ref, refs[:-1])


def keep_columns(lay, place_ref, seg_one, seg_two, parent, level_row, value):
    parts = [None] * (value.shape[1] // lay.width)
    for index, column in lay.blocks(value.shape[1] // lay.width):
        above = parent[seg_two[lay.column_id(column, place_ref[1])]]
        parts[index] = jnp.where(seg_one[level_row] == above, value[:, lay.lanes(index)], 0.0)
    return jnp.concatenate(parts, axis=1)


def level_slot(level_refs, slot):
    half = level_refs[0].shape[0]
    return level_refs[slot // half][slot % half]


def level_two_kernel(lay, weight, groups, level_groups, pieces, place_ref, seg_one, seg_two, parent, solved_ref, *refs):
    level_refs, piece_refs = refs[:2], refs[2 : 2 + pieces]
    out_ref, panel_ref = refs[-2:]
    fill_panel(piece_refs, panel_ref)
    width = lay.width
    depth = solved_ref.shape[1]
    columns = level_refs[0].shape[2]
    total = jnp.zeros((level_groups * width, columns), F32)
    for slot in range(lay.prow):
        source = gathered_source(lay, place_ref, slot)
        place, part = lax.rem(source, lay.pcol) ^ place_ref[2], lax.div(source, lay.pcol)
        dinv_parts = []
        for group in range(level_groups):
            start = pl.multiple_of((group * lay.ratio + part) * width, width)
            dinv_parts.append(panel_ref[place, pl.ds(depth + width, width), pl.ds(start, width)])
        dinv_part = jnp.concatenate(dinv_parts, axis=0)
        total = total + product(halves(dinv_part), halves(level_slot(level_refs, slot)))
    extra = jnp.zeros((width, columns), F32)
    for group in range(level_groups):
        level_row = group * lay.prow + place_ref[0]
        lines = total[lay.lanes(group), :]
        extra = extra + keep_columns(lay, place_ref, seg_one, seg_two, parent, level_row, lines)
    left = jnp.concatenate([solved_ref[...], (extra * weight).T], axis=1)
    packed_diagonal(lay, place_ref, seg_two, halves(left), panel_ref, out_ref, groups, weight != 1.0)


def update_kernel(lay, groups, pieces, place_ref, seg_one, seg_two, parent, lower_ref, dinv_ref, *refs):
    level_refs, piece_refs = refs[:2], refs[2 : 2 + pieces]
    out_ref, bundle_ref, panel_ref = refs[-3:]
    fill_panel(piece_refs, panel_ref)
    width = lay.width
    rows = lower_ref.shape[0]
    total = jnp.zeros(lower_ref.shape, F32)
    for slot in range(lay.prow):
        source = gathered_source(lay, place_ref, slot)
        panel_part = panel_columns(lay, panel_ref, slice(None), source, place_ref[2], groups * width)
        value = level_slot(level_refs, slot)
        parts = [
            keep_columns(lay, place_ref, seg_one, seg_two, parent, group * lay.prow + source, value)
            for group in range(groups)
        ]
        total = total + product(halves(panel_part), halves(jnp.concatenate(parts, axis=0)))
    updated = lower_ref[...] - total
    out_ref[...] = updated
    bundle_ref[:rows, :] = updated
    bundle_ref[rows : rows + width, :] = level_slot(level_refs, 0)
    bundle_ref[rows + width :, :] = dinv_ref[...]


def finish_kernel(lay, count, columns, paired, place_ref, segment_ref, diag_ref, dinv_ref, *refs):
    turned_refs, out_ref = refs[:-1], refs[-1]
    prow_place, pcol_place = place_ref[0], place_ref[1]
    groups = columns // lay.ratio
    upper = lax.div(prow_place, lay.pcol)
    for index, column in lay.blocks(columns):
        start = index * lay.width
        if paired:
            part = (index // groups) ^ upper
            start = pl.multiple_of((part * groups + index % groups) * lay.width, lay.width)
        block = diag_ref[pl.ds(start, lay.width), :].T
        for row in range(count):
            value = block
            if paired:
                lines = lay.lanes(row)
                even, odd = (ref[lines, :] for ref in turned_refs)
                value = block + jnp.where(upper == index // groups, even, odd)
            same = (
                segment_ref[row * lay.prow + prow_place]
                == segment_ref[lay.column_id(column, pcol_place)]
            )
            value = jnp.where(same, lay.read(dinv_ref, row, column, columns) + value, 0.0)
            out_ref[pl.ds(row * lay.width * columns + column, lay.width, stride=columns), :] = value


def shift_rows(piece, pairs):
    return lax.ppermute(
        piece, "prow", [(2 * source + core, 2 * target + core) for source, target in pairs for core in range(2)]
    )


def rotations(piece, prow_total):
    chips = prow_total // 2
    return [
        shift_rows(piece, [(chip, (chip + steps) % chips) for chip in range(chips)])
        for steps in range(1, chips)
    ]


def swap_cores(piece, prow_total):
    return lax.ppermute(piece, "prow", [(place, place ^ 1) for place in range(prow_total)])


PAIR_FLOWS = (((1, 0), (3, 1), (0, 2), (2, 3)), ((2, 1), (0, 3)))


def neighbour(piece, flip, pcol_total):
    return lax.ppermute(piece, "pcol", [(place, place ^ flip) for place in range(pcol_total)])


def tied(*values):
    return lax.optimization_barrier(values)


def on_device(
    root_inverse,
    lower_one,
    lower_two,
    dinv_one,
    dinv_two,
    seg_one,
    seg_two,
    parent_two,
    pattern_one,
    pattern_two,
):
    width = root_inverse.shape[2]
    prow_total = lax.axis_size("prow")
    pcol_total = lax.axis_size("pcol")
    prow_place = lax.axis_index("prow").astype(jnp.int32)
    pcol_place = lax.axis_index("pcol").astype(jnp.int32)
    lay = Layout(prow_total, pcol_total, width)
    root_count, root_columns = root_inverse.shape[0], root_inverse.shape[3]
    level_count, one_columns = dinv_one.shape[0], dinv_one.shape[3]
    second_count, two_columns = dinv_two.shape[0], dinv_two.shape[3]
    root_total = pattern_one.shape[1]
    groups_one, groups_two = one_columns // lay.ratio, two_columns // lay.ratio
    counts = (root_count, level_count, one_columns, two_columns, root_total)
    rows = root_count * width
    paired = prow_total == 8 and pcol_total == 4
    flip = pcol_place if paired else jnp.zeros_like(pcol_place)
    place = jnp.stack([prow_place, pcol_place, flip])

    def lines(argument):
        return argument.reshape(-1, width)

    first, level = vmem_call(
        functools.partial(first_kernel, lay, counts),
        (out_shape(rows, one_columns * width), out_shape(width, two_columns * width)),
        [place, seg_one, seg_two, parent_two, pattern_one, pattern_two],
        [lines(lower_one), lines(lower_two)],
    )
    root = vmem_call(
        functools.partial(root_kernel, lay, root_count, root_columns),
        out_shape(rows, root_columns * width),
        [],
        [lines(root_inverse)],
    )

    root_panel = lax.all_gather(root, "pcol", axis=0, tiled=False)

    def start_panel(piece):
        if paired:
            return [neighbour(piece, 1, pcol_total), neighbour(piece, 2, pcol_total)]
        gathered = lax.all_gather(piece, "pcol", axis=0, tiled=False)
        return [gathered[source] for source in range(pcol_total)]

    def end_panel(piece, started):
        if not paired:
            return started
        beside_x, beside_y = started
        middle = piece.shape[0] // 2
        return [
            piece,
            beside_x,
            beside_y,
            neighbour(beside_y[:middle], 1, pcol_total),
            neighbour(beside_x[middle:], 2, pcol_total),
        ]

    def start_slots(piece):
        if paired:
            return [piece] + [shift_rows(piece, flow) for flow in PAIR_FLOWS]
        return [piece] + rotations(piece, prow_total)

    def both_cores(pieces):
        return pieces + [swap_cores(part, prow_total) for part in pieces]

    source_of = paired_source if paired else gathered_source
    weights = [0.5, 1.0, 1.0] * 2 if paired else [1.0] * prow_total

    first_started = start_panel(first)
    level_pieces = rotations(level, prow_total)
    first_later, level_pieces = tied(first, level_pieces)
    first_slots = start_slots(first_later)
    second_root, dinv_packed, level_own = vmem_call(
        functools.partial(second_kernel, lay, counts),
        (
            out_shape(rows, two_columns * width),
            out_shape(width, level_count * lay.ratio * width),
            out_shape(prow_total // 2, width, two_columns * width),
        ),
        [place, seg_two, parent_two, pattern_one, pattern_two],
        [lines(lower_two), lines(dinv_one), level, *level_pieces],
    )
    level_slots = [level_own, swap_cores(level_own, prow_total)]
    first_pieces = end_panel(first, first_started)
    first_pieces, level_slots, first_slots[:-1] = tied(first_pieces, level_slots, first_slots[:-1])
    first_slots = both_cores(first_slots)

    size = rows * one_columns * width
    bundle_rows = rows + 2 * width
    second, bundle = vmem_call(
        functools.partial(update_kernel, lay, groups_one, len(first_pieces)),
        (out_shape(rows, two_columns * width), out_shape(bundle_rows, two_columns * width)),
        [place, seg_one, seg_two, parent_two],
        [second_root, dinv_packed, *level_slots, *first_pieces],
        [pltpu.VMEM((pcol_total, rows, one_columns * width), F32)],
        flops=6 * size * seg_one.shape[0] * width,
    )
    second_slots = start_slots(second)
    bundle, first_slots = tied(bundle, first_slots)
    bundle_started = start_panel(bundle)
    packed_one = vmem_call(
        functools.partial(level_one_kernel, lay, weights, source_of, groups_one, len(first_pieces)),
        out_shape(prow_total, one_columns * width, width),
        [place, seg_one],
        [root_panel, *first_pieces, *first_slots],
        [pltpu.VMEM((pcol_total, rows, one_columns * width), F32)],
        flops=6 * size * (root_total + seg_one.shape[0]) * width,
        after=[second],
    )
    packed_one, second_slots, bundle_started = tied(packed_one, second_slots, bundle_started)
    second_slots = both_cores(second_slots)
    diag_one = lax.psum_scatter(packed_one, "prow", scatter_dimension=0, tiled=False)
    bundle_pieces = end_panel(bundle, bundle_started)
    solved_two = vmem_call(
        functools.partial(solve_two_kernel, lay, weights, source_of),
        out_shape(two_columns * width, rows),
        [place],
        [root_panel, *second_slots],
        flops=6 * size * root_total * width,
    )
    packed_two = vmem_call(
        functools.partial(level_two_kernel, lay, weights[0], groups_two, level_count, len(bundle_pieces)),
        out_shape(prow_total, two_columns * width, width),
        [place, seg_one, seg_two, parent_two],
        [solved_two, *level_slots, *bundle_pieces],
        [pltpu.VMEM((pcol_total, bundle_rows, two_columns * width), F32)],
        flops=6 * size * seg_two.shape[0] * width,
    )
    diag_two = lax.psum_scatter(packed_two, "prow", scatter_dimension=0, tiled=False)

    def partners(diag, groups):
        turned = []
        for turn in range(lay.ratio):
            pairs = []
            for row in range(prow_total):
                part = (row // pcol_total) ^ turn
                for column in range(pcol_total):
                    target = (column + pcol_total * part) * pcol_total + row % pcol_total
                    pairs.append((row * pcol_total + column, target))
            sent = diag[turn * groups * width : (turn + 1) * groups * width]
            turned.append(lax.ppermute(sent, BOTH, pairs))
        return turned

    def finish(dinv, diag, segments, groups):
        count, columns = dinv.shape[0], dinv.shape[3]
        result = vmem_call(
            functools.partial(finish_kernel, lay, count, columns, paired),
            out_shape(count * width * columns, width),
            [place, segments],
            [diag, lines(dinv)] + (partners(diag, groups) if paired else []),
        )
        return result.reshape(dinv.shape)

    return (
        finish(dinv_one, diag_one, seg_one, groups_one),
        finish(dinv_two, diag_two, seg_two, groups_two),
    )


def solution(mesh):
    cyclic = P(None, "prow", None, None, "pcol", None)
    return jax.shard_map(
        on_device,
        mesh=mesh,
        in_specs=(cyclic,) * 5 + (P(),) * 5,
        out_specs=(cyclic, cyclic),
        check_vma=False,
    )
```

time: 1190 us -> 253 us (0.21)
  waiting for transfers between devices: 880 us -> 127 us
  local copies, waits for them, and re-layouts: 181 us -> 6.58 us
  matrix products: 93.1 us -> 0 us
  Pallas kernels: 0 us -> 62.2 us
  starting transfers between devices: 0.58 us -> 42.9 us
  other arithmetic: 13.4 us -> 0.59 us
    unnamed x11 -> x3, waiting for transfers between devices: 575 us -> 0.05 us
    all_gather x4 -> x1, waiting for transfers between devices: 252 us -> 26.4 us  [on_device(): root_panel = lax.all_gather(root, 'pcol', axis=0, tiled=False)]
    dot_general x8 -> x0, matrix products: 93.1 us -> none  [the longest x5 92.5 us: contract(): lax.dot_general(left_side, right_side, (((0,), (0,)), ((), ())), precisio...]
    ppermute x0 -> x26, waiting for transfers between devices: none -> 64.9 us  [the longest x7 44.1 us: shift_rows(): lax.ppermute(piece, 'prow', [(2 * source + core, 2 * target + core) for s...]
    pallas_call x0 -> x9, Pallas kernels: none -> 62.2 us  [vmem_call(): pl.pallas_call(body, out_shape=outs, in_specs=[pl.BlockSpec(memory_space=...]
    all_gather x4 -> x0, local copies, waits for them, and re-layouts: 52.6 us -> none  [the longest x1 23.8 us: on_device(): lax.all_gather(to_blocks(region, block_width), 'pcol', axis=4, tiled=True)]
    another operation x5 -> x0, local copies, waits for them, and re-layouts: 48.1 us -> none  [the longest x4 46 us: row_panel(): picked.reshape(picked.shape[0] * picked.shape[1], picked.shape[2] * picke...]
    ppermute x0 -> x26, starting transfers between devices: none -> 42.5 us  [the longest x7 24.1 us: shift_rows(): lax.ppermute(piece, 'prow', [(2 * source + core, 2 * target + core) for s...]
  transfers between devices with their start and end apart: 8 -> 29, of which waited for: 6 -> 14; matrix products, arithmetic and copies ran while one was open for 20% -> 1% of each run, Pallas kernels for 0% -> 22%
where the time goes in v1:
time: 253 us
  waiting for transfers between devices  127 us (50%)
  Pallas kernels  62.2 us (25%)
  starting transfers between devices  42.9 us (17%)
  between operations  14 us (6%)
  local copies, waits for them, and re-layouts  6.58 us (3%)
    pallas_call x9, Pallas kernels, vmem_call(): pl.pallas_call(body, out_shape=outs, in_specs=[pl.BlockSpec(memory_space=...  62.2 us
    ppermute x7, waiting for transfers between devices, shift_rows(): lax.ppermute(piece, 'prow', [(2 * source + core, 2 * target + core) for s...  44.1 us
    reduce_scatter x1, waiting for transfers between devices, on_device(): lax.psum_scatter(packed_two, 'prow', scatter_dimension=0, tiled=False)  33.6 us
    all_gather x1, waiting for transfers between devices, on_device(): root_panel = lax.all_gather(root, 'pcol', axis=0, tiled=False)  26.4 us
    ppermute x7, starting transfers between devices, shift_rows(): lax.ppermute(piece, 'prow', [(2 * source + core, 2 * target + core) for s...  24.1 us
    ppermute x8, starting transfers between devices, neighbour(): lax.ppermute(piece, 'pcol', [(place, place ^ flip) for place in range(pco...  10.6 us
    ppermute x8, waiting for transfers between devices, neighbour(): lax.ppermute(piece, 'pcol', [(place, place ^ flip) for place in range(pco...  9.5 us
    ppermute x4, waiting for transfers between devices, partners(): turned.append(lax.ppermute(sent, BOTH, pairs))  8.33 us
  transfers between devices with their start and end apart: 29, of which 14 were waited for; matrix products, arithmetic and copies ran while one was open for 1% of the time, Pallas kernels for 22%

profile of v1, /device:TPU:4, one launch (start us, length us, event | category | flops | bytes accessed | tf_op | source)
XLA Modules:
  0.0 253.1 jit_solution(14779932301576180927)
XLA Ops:
  7.2 3.4 %shard_map.116 = f32[512,1024]{1,0:T(8,128)} custom-call(f32[4096,128]{1,0:T(8,128)} %bitcast.26), custom_call_target="tpu_custom_call" | custom-call | bytes 2097152 | tf_op jit(solution)/shard_map/pallas_call | solution.py:32
  10.7 0.6 pad_add_fusion.refs_0_.refs_1_
  11.3 3.0 %shard_map.113 = (f32[512,512]{1,0:T(8,128)}, f32[128,512]{1,0:T(8,128)}) custom-call(s32[3]{0:T(128)} %pad_add_fusion.refs_0_.refs_1_, s32[16]{0:T(128)} %refs_1_.10, s32[16]{0:T(128)} %refs_1_.11, s32[4]{0:T(128)} %refs_3_.7, s32[3,32]{1,0:T(4,128)} %refs_3_.5, s32[4,48]{1,0:T(4,128)} %refs_4_.3, f32[2048,128]{1,0:T(8,128)} %bitcast.29, f32[3072,128]{1,0:T(8,128)} %bitcast.24), custom_call_target="tpu_custom_call" | custom-call | bytes 2621440 | tf_op jit(solution)/shard_map/pallas_call | solution.py:32
  14.2 2.0 collective-permute-start.3
  16.2 1.6 collective-permute-start
  17.8 2.6 %collective-permute-start.1 = (f32[128,512]{1,0:T(8,128)}, f32[128,512]{1,0:T(8,128)S(1)}, u32[]{:S(2)}, u32[]{:S(2)}) collective-permute-start(f32[128,512]{1,0:T(8,128)} %get-tuple-element.35.refs_7_), channel_id=1, source_target_pairs={{0,16},{4,20},{8,24},{12,28},{16,0},{20,4},{24,8},{28,12},{1,17},{... | collective-permute-start | bytes 786440 | tf_op jit(solution)/shard_map/ppermute | solution.py:294
  20.4 1.3 collective-permute-start.2
  21.7 5.9 %collective-permute-done.refs_8_ = f32[128,512]{1,0:T(8,128)S(1)} collective-permute-done((f32[128,512]{1,0:T(8,128)}, f32[128,512]{1,0:T(8,128)S(1)}, u32[]{:S(2)}, u32[]{:S(2)}) %collective-permute-start) | collective-permute-done | bytes 262176 | tf_op jit(solution)/shard_map/ppermute | solution.py:294
  27.6 9.5 %collective-permute-done.1.refs_9_ = f32[128,512]{1,0:T(8,128)S(1)} collective-permute-done((f32[128,512]{1,0:T(8,128)}, f32[128,512]{1,0:T(8,128)S(1)}, u32[]{:S(2)}, u32[]{:S(2)}) %collective-permute-start.1) | collective-permute-done | bytes 262176 | tf_op jit(solution)/shard_map/ppermute | solution.py:294
  37.1 9.1 %collective-permute-start.9 = (f32[512,512]{1,0:T(8,128)}, f32[512,512]{1,0:T(8,128)S(1)}, u32[]{:S(2)}, u32[]{:S(2)}) collective-permute-start(f32[512,512]{1,0:T(8,128)} %get-tuple-element.55.refs_8_.refs_4_.refs_9_), channel_id=1, source_target_pairs={{16,8},{20,12},{0,24},{4,28},{17,9},{21,13},{1,25},{5,29},{18,10},... | collective-permute-start | bytes 3145736 | tf_op jit(solution)/shard_map/ppermute | solution.py:294
  46.3 3.4 %shard_map.114 = (f32[512,512]{1,0:T(8,128)}, f32[128,512]{1,0:T(8,128)}, f32[4,128,512]{2,1,0:T(8,128)}) custom-call(s32[3]{0:T(128)} %pad_add_fusion.refs_0_.refs_1_, s32[16]{0:T(128)} %refs_1_.11, s32[4]{0:T(128)} %refs_3_.7, s32[3,32]{1,0:T(4,128)} %refs_3_.5, s32[4,48]{1,0:T(4,128)} %refs_4_.3, f32[3072,128]{1,0:T(8,128)} %bitcast.25, ...), custom_call_target="tpu_custom_call" | custom-call | bytes 3145728 | tf_op jit(solution)/shard_map/pallas_call | solution.py:32
  49.7 0.5 collective-permute-start.8
  50.1 6.5 %collective-permute-done.4.refs_10_.refs_6_ = f32[512,512]{1,0:T(8,128)S(1)} collective-permute-done((f32[512,512]{1,0:T(8,128)}, f32[512,512]{1,0:T(8,128)S(1)}, u32[]{:S(2)}, u32[]{:S(2)}) %collective-permute-start.4) | collective-permute-done | bytes 1048608 | tf_op jit(solution)/shard_map/ppermute | solution.py:315
  56.7 1.3 collective-permute-start.5
  58.1 3.0 %collective-permute-start.6 = (f32[256,512]{1,0:T(8,128)S(1)}, f32[256,512]{1,0:T(8,128)S(1)}, u32[]{:S(2)}, u32[]{:S(2)}) collective-permute-start(f32[256,512]{1,0:T(8,128)S(1)} %slice.49), channel_id=1, source_target_pairs={{0,2},{1,3},{2,0},{3,1},{4,6},{5,7},{6,4},{7,5},{8,10},{9,11},{10,... | collective-permute-start | bytes 1572872 | tf_op jit(solution)/shard_map/ppermute | solution.py:315
  61.1 9.0 %collective-permute-done.9.refs_11_ = f32[512,512]{1,0:T(8,128)S(1)} collective-permute-done((f32[512,512]{1,0:T(8,128)}, f32[512,512]{1,0:T(8,128)S(1)}, u32[]{:S(2)}, u32[]{:S(2)}) %collective-permute-start.9) | collective-permute-done | bytes 1048608 | tf_op jit(solution)/shard_map/ppermute | solution.py:294
  70.1 19.7 %collective-permute-done.8.refs_10_ = f32[512,512]{1,0:T(8,128)S(1)} collective-permute-done((f32[512,512]{1,0:T(8,128)S(1)}, f32[512,512]{1,0:T(8,128)S(1)}, u32[]{:S(2)}, u32[]{:S(2)}) %collective-permute-start.8) | collective-permute-done | bytes 1048608 | tf_op jit(solution)/shard_map/ppermute | solution.py:294
  89.9 0.9 copy-done.20
  90.8 8.4 %shard_map.115 = (f32[512,512]{1,0:T(8,128)}, f32[768,512]{1,0:T(8,128)}) custom-call(s32[3]{0:T(128)} %pad_add_fusion.refs_0_.refs_1_, s32[16]{0:T(128)} %refs_1_.10, s32[16]{0:T(128)} %refs_1_.11, s32[4]{0:T(128)} %refs_3_.7, f32[512,512]{1,0:T(8,128)} %get-tuple-element.40.refs_4_, f32[128,512]{1,0:T(8,128)} %get-tuple-element.41.refs_5_, ...), custom_call_target="tpu_custom_call" | custom-call | flops 3221225472 | bytes 7602176 | tf_op jit(solution)/shard_map/pallas_call | solution.py:32
  99.3 1.0 copy-done.15
  100.3 0.5 collective-permute-start.15
  100.8 1.5 collective-permute-start.16
  102.3 3.4 %collective-permute-start.13 = (f32[512,512]{1,0:T(8,128)}, f32[512,512]{1,0:T(8,128)}, u32[]{:S(2)}, u32[]{:S(2)}) collective-permute-start(f32[512,512]{1,0:T(8,128)} %get-tuple-element.63.refs_0_.refs_2_), channel_id=1, source_target_pairs={{8,0},{12,4},{24,8},{28,12},{0,16},{4,20},{16,24},{20,28},{9,1},{1... | collective-permute-start | bytes 3145736 | tf_op jit(solution)/shard_map/ppermute | solution.py:294
  105.8 5.6 %collective-permute-start.14 = (f32[512,512]{1,0:T(8,128)}, f32[512,512]{1,0:T(8,128)}, u32[]{:S(2)}, u32[]{:S(2)}) collective-permute-start(f32[512,512]{1,0:T(8,128)} %get-tuple-element.63.refs_0_.refs_2_), channel_id=1, source_target_pairs={{16,8},{20,12},{0,24},{4,28},{17,9},{21,13},{1,25},{5,29},{18,10},... | collective-permute-start | bytes 3145736 | tf_op jit(solution)/shard_map/ppermute | solution.py:294
  111.3 26.4 %all-gather.3.cloned.1.call-done = f32[2048,1024]{1,0:T(8,128)} async-done(((f32[512,1024]{1,0:T(8,128)}), f32[2048,1024]{1,0:T(8,128)}) %all-gather.3.cloned.1.call-update) | async-done | bytes 8388624 | tf_op jit(solution)/shard_map/all_gather | solution.py:367
  137.7 16.2 %shard_map.117 = f32[8,512,128]{2,1,0:T(8,128)} custom-call(f32[512,512]{1,0:T(8,128)} %get-tuple-element.63.refs_0_.refs_2_, s32[3]{0:T(128)} %pad_add_fusion.refs_0_.refs_1_, s32[16]{0:T(128)} %refs_1_.10, f32[4,512,1024]{2,1,0:T(8,128)} %bitcast.35, f32[512,512]{1,0:T(8,128)} %get-tuple-element.55.refs_8_.refs_4_.refs_9_, f32[512,512]{1,0:T(8,128)} %copy-done.6, ...), custom_call_target="tpu_custom_call" | custom-call | flops 9663676416 | bytes 18874368 | tf_op jit(solution)/shard_map/pallas_call | solution.py:32
  154.5 0.5 collective-permute-start.20
  155.2 0.6 collective-permute-start.22
  155.9 1.5 collective-permute-start.23
  157.4 1.5 collective-permute-done.20.refs_6_
  158.9 1.5 collective-permute-done.21.refs_7_
  160.4 1.1 copy-done.18
  161.5 11.4 %shard_map.119.refs_4_ = f32[512,512]{1,0:T(8,128)} custom-call(s32[3]{0:T(128)} %pad_add_fusion.refs_0_.refs_1_, f32[4,512,1024]{2,1,0:T(8,128)} %bitcast.36, f32[512,512]{1,0:T(8,128)} %get-tuple-element.63.refs_0_.refs_2_, f32[512,512]{1,0:T(8,128)} %collective-permute-done.13.refs_3_, f32[512,512]{1,0:T(8,128)} %collective-permute-done.14.refs_4_, ...), custom_call_target="tpu_custom_call" | custom-call | flops 6442450944 | bytes 14680064 | tf_op jit(solution)/shard_map/pallas_call | solution.py:32
  172.9 2.4 collective-permute-done.22.refs_10_
  175.7 12.2 %shard_map.120 = f32[8,512,128]{2,1,0:T(8,128)} custom-call(s32[3]{0:T(128)} %pad_add_fusion.refs_0_.refs_1_, s32[16]{0:T(128)} %refs_1_.10, s32[16]{0:T(128)} %refs_1_.11, s32[4]{0:T(128)} %refs_3_.7, f32[512,512]{1,0:T(8,128)} %shard_map.119.refs_4_, f32[4,128,512]{2,1,0:T(8,128)} %get-tuple-element.44.refs_6_.refs_5_, f32[4,128,512]{2,1,0:T(8,128)} %copy-done.11, ...), custom_call_target="tpu_custom_call" | custom-call | flops 3221225472 | bytes 9437184 | tf_op jit(solution)/shard_map/pallas_call | solution.py:32
  187.9 2.0 reduce-scatter.3.cloned.1.call-done
  189.8 1.0 slice_bitcast_fusion.2
  190.8 2.3 collective-permute-start.17
  193.2 2.5 collective-permute-start.18
  195.6 33.6 %reduce-scatter.5.cloned.1.call-done = f32[1,512,128]{2,1,0:T(8,128)} async-done(((f32[8,512,128]{2,1,0:T(8,128)}), f32[1,512,128]{2,1,0:T(8,128)}) %reduce-scatter.5.cloned.1.call-update) | async-done | bytes 262160 | tf_op jit(solution)/shard_map/reduce_scatter | solution.py:459
  229.2 1.0 slice_bitcast_fusion
  230.2 1.9 collective-permute-start.24
  232.2 0.5 collective-permute-start.25
  232.7 0.6 copy-done.7
  233.3 2.1 shard_map.118
  235.5 8.3 %collective-permute-done.24.refs_4_ = f32[256,128]{1,0:T(8,128)S(1)} collective-permute-done((f32[256,128]{1,0:T(8,128)S(1)}, f32[256,128]{1,0:T(8,128)S(1)}, u32[]{:S(2)}, u32[]{:S(2)}) %collective-permute-start.24) | collective-permute-done | bytes 131104 | tf_op jit(solution)/shard_map/ppermute | solution.py:471
  243.8 0.7 copy-done.8
  244.5 2.1 shard_map.121
  (71 shorter events, 1.7 us)
Async XLA Ops:
  7.2 130.6 %all-gather.3.cloned.1.call-start = ((), (), s32[]{:S(2)}) async-start(), calls=%async_computation.4 | async-start | bytes 10485760 | tf_op jit(solution)/shard_map/all_gather | solution.py:367
  10.6 179.2 %reduce-scatter.3.cloned.1.call-start = ((), (), s32[]{:S(2)}) async-start(), calls=%async_computation.2 | async-start | bytes 2359296 | tf_op jit(solution)/shard_map/reduce_scatter | solution.py:442
  14.2 35.4 %copy-start.12 = (f32[512,512]{1,0:T(8,128)S(1)}, f32[512,512]{1,0:T(8,128)}, u32[]{:S(2)}) copy-start(f32[512,512]{1,0:T(8,128)} %get-tuple-element.55.refs_8_.refs_4_.refs_9_) | copy-start | bytes 3145732
  14.2 42.4 %collective-permute-start.4 = (f32[512,512]{1,0:T(8,128)}, f32[512,512]{1,0:T(8,128)S(1)}, u32[]{:S(2)}, u32[]{:S(2)}) collective-permute-start(f32[512,512]{1,0:T(8,128)} %get-tuple-element.55.refs_8_.refs_4_.refs_9_), channel_id=1, source_target_pairs={{0,2},{1,3},{2,0},{3,1},{4,6},{5,7},{6,4},{7,5},{8,10},{9,11},{10,... | collective-permute-start | bytes 3145736 | tf_op jit(solution)/shard_map/ppermute | solution.py:315
  14.2 43.8 %collective-permute-start.3 = (f32[512,512]{1,0:T(8,128)}, f32[512,512]{1,0:T(8,128)S(1)}, u32[]{:S(2)}, u32[]{:S(2)}) collective-permute-start(f32[512,512]{1,0:T(8,128)} %get-tuple-element.55.refs_8_.refs_4_.refs_9_), channel_id=1, source_target_pairs={{0,1},{1,0},{2,3},{3,2},{4,5},{5,4},{6,7},{7,6},{8,9},{9,8},{10,11... | collective-permute-start | bytes 3145736 | tf_op jit(solution)/shard_map/ppermute | solution.py:315
  16.2 11.4 %collective-permute-start = (f32[128,512]{1,0:T(8,128)}, f32[128,512]{1,0:T(8,128)S(1)}, u32[]{:S(2)}, u32[]{:S(2)}) collective-permute-start(f32[128,512]{1,0:T(8,128)} %get-tuple-element.35.refs_7_), channel_id=1, source_target_pairs={{0,8},{4,12},{8,16},{12,20},{16,24},{20,28},{24,0},{28,4},{1,9},{5... | collective-permute-start | bytes 786440 | tf_op jit(solution)/shard_map/ppermute | solution.py:294
  17.8 19.3 %collective-permute-start.1 = (f32[128,512]{1,0:T(8,128)}, f32[128,512]{1,0:T(8,128)S(1)}, u32[]{:S(2)}, u32[]{:S(2)}) collective-permute-start(f32[128,512]{1,0:T(8,128)} %get-tuple-element.35.refs_7_), channel_id=1, source_target_pairs={{0,16},{4,20},{8,24},{12,28},{16,0},{20,4},{24,8},{28,12},{1,17},{... | collective-permute-start | bytes 786440 | tf_op jit(solution)/shard_map/ppermute | solution.py:294
  20.4 16.8 %collective-permute-start.2 = (f32[128,512]{1,0:T(8,128)}, f32[128,512]{1,0:T(8,128)S(1)}, u32[]{:S(2)}, u32[]{:S(2)}) collective-permute-start(f32[128,512]{1,0:T(8,128)} %get-tuple-element.35.refs_7_), channel_id=1, source_target_pairs={{0,24},{4,28},{8,0},{12,4},{16,8},{20,12},{24,16},{28,20},{1,25},{... | collective-permute-start | bytes 786440 | tf_op jit(solution)/shard_map/ppermute | solution.py:294
  27.6 18.6 %copy-start.2 = (f32[128,512]{1,0:T(8,128)}, f32[128,512]{1,0:T(8,128)S(1)}, u32[]{:S(2)}) copy-start(f32[128,512]{1,0:T(8,128)S(1)} %collective-permute-done.refs_8_) | copy-start | bytes 786436
  37.1 9.1 %copy-start.3 = (f32[128,512]{1,0:T(8,128)}, f32[128,512]{1,0:T(8,128)S(1)}, u32[]{:S(2)}) copy-start(f32[128,512]{1,0:T(8,128)S(1)} %collective-permute-done.1.refs_9_) | copy-start | bytes 786436
  37.1 9.1 %copy-start.4 = (f32[128,512]{1,0:T(8,128)}, f32[128,512]{1,0:T(8,128)S(1)}, u32[]{:S(2)}) copy-start(f32[128,512]{1,0:T(8,128)S(1)} %collective-permute-done.2.refs_10_) | copy-start | bytes 786436
  37.1 32.9 %collective-permute-start.9 = (f32[512,512]{1,0:T(8,128)}, f32[512,512]{1,0:T(8,128)S(1)}, u32[]{:S(2)}, u32[]{:S(2)}) collective-permute-start(f32[512,512]{1,0:T(8,128)} %get-tuple-element.55.refs_8_.refs_4_.refs_9_), channel_id=1, source_target_pairs={{16,8},{20,12},{0,24},{4,28},{17,9},{21,13},{1,25},{5,29},{18,10},... | collective-permute-start | bytes 3145736 | tf_op jit(solution)/shard_map/ppermute | solution.py:294
  49.6 20.4 %collective-permute-start.7 = (f32[4,128,512]{2,1,0:T(8,128)}, f32[4,128,512]{2,1,0:T(8,128)S(1)}, u32[]{:S(2)}, u32[]{:S(2)}) collective-permute-start(f32[4,128,512]{2,1,0:T(8,128)} %get-tuple-element.44.refs_6_.refs_5_), channel_id=1, source_target_pairs={{0,4},{4,0},{8,12},{12,8},{16,20},{20,16},{24,28},{28,24},{1,5},{5... | collective-permute-start | bytes 3145736 | tf_op jit(solution)/shard_map/ppermute | solution.py:308
  49.7 40.1 %collective-permute-start.8 = (f32[512,512]{1,0:T(8,128)S(1)}, f32[512,512]{1,0:T(8,128)S(1)}, u32[]{:S(2)}, u32[]{:S(2)}) collective-permute-start(f32[512,512]{1,0:T(8,128)S(1)} %copy-done.12), channel_id=1, source_target_pairs={{8,0},{12,4},{24,8},{28,12},{0,16},{4,20},{16,24},{20,28},{9,1},{1... | collective-permute-start | bytes 3145736 | tf_op jit(solution)/shard_map/ppermute | solution.py:294
  56.6 34.2 %copy-start.5 = (f32[512,512]{1,0:T(8,128)}, f32[512,512]{1,0:T(8,128)S(1)}, u32[]{:S(2)}) copy-start(f32[512,512]{1,0:T(8,128)S(1)} %collective-permute-done.4.refs_10_.refs_6_) | copy-start | bytes 3145732
  56.7 33.1 %collective-permute-start.5 = (f32[256,512]{1,0:T(8,128)S(1)}, f32[256,512]{1,0:T(8,128)S(1)}, u32[]{:S(2)}, u32[]{:S(2)}) collective-permute-start(f32[256,512]{1,0:T(8,128)S(1)} %slice.48), channel_id=1, source_target_pairs={{0,1},{1,0},{2,3},{3,2},{4,5},{5,4},{6,7},{7,6},{8,9},{9,8},{10,11... | collective-permute-start | bytes 1572872 | tf_op jit(solution)/shard_map/ppermute | solution.py:315
  58.0 32.8 %copy-start.6 = (f32[512,512]{1,0:T(8,128)}, f32[512,512]{1,0:T(8,128)S(1)}, u32[]{:S(2)}) copy-start(f32[512,512]{1,0:T(8,128)S(1)} %collective-permute-done.3.refs_9_.refs_5_) | copy-start | bytes 3145732
  58.1 31.7 %collective-permute-start.6 = (f32[256,512]{1,0:T(8,128)S(1)}, f32[256,512]{1,0:T(8,128)S(1)}, u32[]{:S(2)}, u32[]{:S(2)}) collective-permute-start(f32[256,512]{1,0:T(8,128)S(1)} %slice.49), channel_id=1, source_target_pairs={{0,2},{1,3},{2,0},{3,1},{4,6},{5,7},{6,4},{7,5},{8,10},{9,11},{10,... | collective-permute-start | bytes 1572872 | tf_op jit(solution)/shard_map/ppermute | solution.py:315
  70.1 29.2 %copy-start.13 = (f32[512,512]{1,0:T(8,128)}, f32[512,512]{1,0:T(8,128)S(1)}, u32[]{:S(2)}) copy-start(f32[512,512]{1,0:T(8,128)S(1)} %collective-permute-done.9.refs_11_) | copy-start | bytes 3145732
  70.1 29.2 %collective-permute-start.12 = (f32[512,512]{1,0:T(8,128)S(1)}, f32[512,512]{1,0:T(8,128)S(1)}, u32[]{:S(2)}, u32[]{:S(2)}) collective-permute-start(f32[512,512]{1,0:T(8,128)S(1)} %collective-permute-done.9.refs_11_), channel_id=1, source_target_pairs={{0,4},{4,0},{8,12},{12,8},{16,20},{20,16},{24,28},{28,24},{1,5},{5... | collective-permute-start | bytes 3145736 | tf_op jit(solution)/shard_map/ppermute | solution.py:308
  70.1 20.7 %copy-start.11 = (f32[4,128,512]{2,1,0:T(8,128)}, f32[4,128,512]{2,1,0:T(8,128)S(1)}, u32[]{:S(2)}) copy-start(f32[4,128,512]{2,1,0:T(8,128)S(1)} %collective-permute-done.7.refs_7_.refs_6_) | copy-start | bytes 3145732
  89.8 9.5 %copy-start.14 = (f32[512,512]{1,0:T(8,128)}, f32[512,512]{1,0:T(8,128)S(1)}, u32[]{:S(2)}) copy-start(f32[512,512]{1,0:T(8,128)S(1)} %collective-permute-done.8.refs_10_) | copy-start | bytes 3145732
  89.8 1.1 copy-start.19
  89.8 1.0 copy-start.20
  89.8 9.5 %collective-permute-start.10 = (f32[512,512]{1,0:T(8,128)S(1)}, f32[512,512]{1,0:T(8,128)}, u32[]{:S(2)}, u32[]{:S(2)}) collective-permute-start(f32[512,512]{1,0:T(8,128)S(1)} %copy-done.12), channel_id=1, source_target_pairs={{0,4},{4,0},{8,12},{12,8},{16,20},{20,16},{24,28},{28,24},{1,5},{5... | collective-permute-start | bytes 3145736 | tf_op jit(solution)/shard_map/ppermute | solution.py:308
  90.8 8.5 %collective-permute-start.11 = (f32[512,512]{1,0:T(8,128)S(1)}, f32[512,512]{1,0:T(8,128)}, u32[]{:S(2)}, u32[]{:S(2)}) collective-permute-start(f32[512,512]{1,0:T(8,128)S(1)} %collective-permute-done.8.refs_10_), channel_id=1, source_target_pairs={{0,4},{4,0},{8,12},{12,8},{16,20},{20,16},{24,28},{28,24},{1,5},{5... | collective-permute-start | bytes 3145736 | tf_op jit(solution)/shard_map/ppermute | solution.py:308
  99.2 1.1 copy-start.15
  100.3 53.9 %collective-permute-start.15 = (f32[768,512]{1,0:T(8,128)}, f32[768,512]{1,0:T(8,128)S(1)}, u32[]{:S(2)}, u32[]{:S(2)}) collective-permute-start(f32[768,512]{1,0:T(8,128)} %get-tuple-element.61.refs_7_), channel_id=1, source_target_pairs={{0,1},{1,0},{2,3},{3,2},{4,5},{5,4},{6,7},{7,6},{8,9},{9,8},{10,11... | collective-permute-start | bytes 4718600 | tf_op jit(solution)/shard_map/ppermute | solution.py:315
  100.8 53.3 %collective-permute-start.16 = (f32[768,512]{1,0:T(8,128)}, f32[768,512]{1,0:T(8,128)S(1)}, u32[]{:S(2)}, u32[]{:S(2)}) collective-permute-start(f32[768,512]{1,0:T(8,128)} %get-tuple-element.61.refs_7_), channel_id=1, source_target_pairs={{0,2},{1,3},{2,0},{3,1},{4,6},{5,7},{6,4},{7,5},{8,10},{9,11},{10,... | collective-permute-start | bytes 4718600 | tf_op jit(solution)/shard_map/ppermute | solution.py:315
  102.3 51.6 %collective-permute-start.13 = (f32[512,512]{1,0:T(8,128)}, f32[512,512]{1,0:T(8,128)}, u32[]{:S(2)}, u32[]{:S(2)}) collective-permute-start(f32[512,512]{1,0:T(8,128)} %get-tuple-element.63.refs_0_.refs_2_), channel_id=1, source_target_pairs={{8,0},{12,4},{24,8},{28,12},{0,16},{4,20},{16,24},{20,28},{9,1},{1... | collective-permute-start | bytes 3145736 | tf_op jit(solution)/shard_map/ppermute | solution.py:294
  105.8 48.1 %collective-permute-start.14 = (f32[512,512]{1,0:T(8,128)}, f32[512,512]{1,0:T(8,128)}, u32[]{:S(2)}, u32[]{:S(2)}) collective-permute-start(f32[512,512]{1,0:T(8,128)} %get-tuple-element.63.refs_0_.refs_2_), channel_id=1, source_target_pairs={{16,8},{20,12},{0,24},{4,28},{17,9},{21,13},{1,25},{5,29},{18,10},... | collective-permute-start | bytes 3145736 | tf_op jit(solution)/shard_map/ppermute | solution.py:294
  154.2 1.7 copy-start
  154.2 1.7 copy-start.1
  154.2 75.0 %reduce-scatter.5.cloned.1.call-start = ((), (), s32[]{:S(2)}) async-start(), calls=%async_computation.3 | async-start | bytes 2359296 | tf_op jit(solution)/shard_map/reduce_scatter | solution.py:459
  154.5 2.9 %collective-permute-start.19 = (f32[512,512]{1,0:T(8,128)}, f32[512,512]{1,0:T(8,128)S(1)}, u32[]{:S(2)}, u32[]{:S(2)}) collective-permute-start(f32[512,512]{1,0:T(8,128)} %get-tuple-element.63.refs_0_.refs_2_), channel_id=1, source_target_pairs={{0,4},{4,0},{8,12},{12,8},{16,20},{20,16},{24,28},{28,24},{1,5},{5... | collective-permute-start | bytes 3145736 | tf_op jit(solution)/shard_map/ppermute | solution.py:308
  154.5 4.4 %collective-permute-start.20 = (f32[512,512]{1,0:T(8,128)}, f32[512,512]{1,0:T(8,128)S(1)}, u32[]{:S(2)}, u32[]{:S(2)}) collective-permute-start(f32[512,512]{1,0:T(8,128)} %collective-permute-done.13.refs_3_), channel_id=1, source_target_pairs={{0,4},{4,0},{8,12},{12,8},{16,20},{20,16},{24,28},{28,24},{1,5},{5... | collective-permute-start | bytes 3145736 | tf_op jit(solution)/shard_map/ppermute | solution.py:308
  155.0 5.4 %collective-permute-start.21 = (f32[512,512]{1,0:T(8,128)}, f32[512,512]{1,0:T(8,128)S(1)}, u32[]{:S(2)}, u32[]{:S(2)}) collective-permute-start(f32[512,512]{1,0:T(8,128)} %collective-permute-done.14.refs_4_), channel_id=1, source_target_pairs={{0,4},{4,0},{8,12},{12,8},{16,20},{20,16},{24,28},{28,24},{1,5},{5... | collective-permute-start | bytes 3145736 | tf_op jit(solution)/shard_map/ppermute | solution.py:308
  155.2 20.1 %collective-permute-start.22 = (f32[384,512]{1,0:T(8,128)S(1)}, f32[384,512]{1,0:T(8,128)}, u32[]{:S(2)}, u32[]{:S(2)}) collective-permute-start(f32[384,512]{1,0:T(8,128)S(1)} %slice.42), channel_id=1, source_target_pairs={{0,1},{1,0},{2,3},{3,2},{4,5},{5,4},{6,7},{7,6},{8,9},{9,8},{10,11... | collective-permute-start | bytes 2359304 | tf_op jit(solution)/shard_map/ppermute | solution.py:315
  155.9 19.8 %collective-permute-start.23 = (f32[384,512]{1,0:T(8,128)S(1)}, f32[384,512]{1,0:T(8,128)}, u32[]{:S(2)}, u32[]{:S(2)}) collective-permute-start(f32[384,512]{1,0:T(8,128)S(1)} %slice.43), channel_id=1, source_target_pairs={{0,2},{1,3},{2,0},{3,1},{4,6},{5,7},{6,4},{7,5},{8,10},{9,11},{10,... | collective-permute-start | bytes 2359304 | tf_op jit(solution)/shard_map/ppermute | solution.py:315
  157.4 3.0 %copy-start.16 = (f32[512,512]{1,0:T(8,128)}, f32[512,512]{1,0:T(8,128)S(1)}, u32[]{:S(2)}) copy-start(f32[512,512]{1,0:T(8,128)S(1)} %collective-permute-done.19.refs_5_) | copy-start | bytes 3145732
  158.9 1.5 copy-start.17
  160.4 1.1 copy-start.18
  190.8 41.8 %collective-permute-start.17 = (f32[256,128]{1,0:T(8,128)S(1)}, f32[256,128]{1,0:T(8,128)S(1)}, u32[]{:S(2)}, u32[]{:S(2)}) collective-permute-start(f32[256,128]{1,0:T(8,128)S(1)} %get-tuple-element.73), channel_id=1, source_target_pairs={{0,0},{1,4},{2,8},{3,12},{4,1},{5,5},{6,9},{7,13},{8,2},{9,6},{10,... | collective-permute-start | bytes 393224 | tf_op jit(solution)/shard_map/ppermute | solution.py:471
  193.2 39.5 %collective-permute-start.18 = (f32[256,128]{1,0:T(8,128)S(1)}, f32[256,128]{1,0:T(8,128)S(1)}, u32[]{:S(2)}, u32[]{:S(2)}) collective-permute-start(f32[256,128]{1,0:T(8,128)S(1)} %get-tuple-element.72), channel_id=1, source_target_pairs={{0,16},{1,20},{2,24},{3,28},{4,17},{5,21},{6,25},{7,29},{8,18},{9,... | collective-permute-start | bytes 393224 | tf_op jit(solution)/shard_map/ppermute | solution.py:471
  230.2 13.6 %collective-permute-start.24 = (f32[256,128]{1,0:T(8,128)S(1)}, f32[256,128]{1,0:T(8,128)S(1)}, u32[]{:S(2)}, u32[]{:S(2)}) collective-permute-start(f32[256,128]{1,0:T(8,128)S(1)} %get-tuple-element.71), channel_id=1, source_target_pairs={{0,0},{1,4},{2,8},{3,12},{4,1},{5,5},{6,9},{7,13},{8,2},{9,6},{10,... | collective-permute-start | bytes 393224 | tf_op jit(solution)/shard_map/ppermute | solution.py:471
  232.2 11.6 %collective-permute-start.25 = (f32[256,128]{1,0:T(8,128)S(1)}, f32[256,128]{1,0:T(8,128)S(1)}, u32[]{:S(2)}, u32[]{:S(2)}) collective-permute-start(f32[256,128]{1,0:T(8,128)S(1)} %get-tuple-element.70), channel_id=1, source_target_pairs={{0,16},{1,20},{2,24},{3,28},{4,17},{5,21},{6,25},{7,29},{8,18},{9,... | collective-permute-start | bytes 393224 | tf_op jit(solution)/shard_map/ppermute | solution.py:471
  232.6 0.7 copy-start.9
  243.8 0.7 copy-start.10
  (2 other events, 1.3 us)
Sparse Core Ops, SparseCore 0:
  10.7 126.9 all-gather.2
  154.3 35.4 reduce-scatter.2
  192.1 37.0 reduce-scatter.4

commit v2 on v1

--- a/solution.py
+++ b/solution.py
@@ -25,7 +25,7 @@
     return dot(left_high, right_high) + (dot(left_high, right_low) + dot(left_low, right_high))
 
 
-def vmem_call(kernel, outs, smem_args, vmem_args, scratch=(), flops=0, after=()):
+def vmem_call(kernel, outs, smem_args, vmem_args, any_args=(), scratch=(), flops=0, after=()):
     def body(*refs):
         kernel(*refs[len(after) :])
 
@@ -34,16 +34,17 @@
         out_shape=outs,
         in_specs=[pl.BlockSpec(memory_space=pl.ANY)] * len(after)
         + [pl.BlockSpec(memory_space=pltpu.SMEM)] * len(smem_args)
-        + [pl.BlockSpec(memory_space=pltpu.VMEM)] * len(vmem_args),
+        + [pl.BlockSpec(memory_space=pltpu.VMEM)] * len(vmem_args)
+        + [pl.BlockSpec(memory_space=pl.ANY)] * len(any_args),
         out_specs=jax.tree.map(lambda _: pl.BlockSpec(memory_space=pltpu.VMEM), outs),
         scratch_shapes=scratch,
         compiler_params=pltpu.CompilerParams(vmem_limit_bytes=VMEM_LIMIT),
         cost_estimate=pl.CostEstimate(
             flops=flops,
-            bytes_accessed=sum(4 * arg.size for arg in vmem_args),
+            bytes_accessed=sum(4 * arg.size for arg in (*vmem_args, *any_args)),
             transcendentals=0,
         ),
-    )(*after, *smem_args, *vmem_args)
+    )(*after, *smem_args, *vmem_args, *any_args)
 
 
 def out_shape(*dims):
@@ -100,11 +101,17 @@
 
 
 def second_kernel(lay, counts, place_ref, seg_two, parent, one, two, lower_two, dinv, *refs):
+    root_count, level_count, one_columns, two_columns, root_total = counts
     level_refs = refs[:-3]
     second_ref, dinv_ref, stack_ref = refs[-3:]
+    for row in range(level_count):
+        for part in range(lay.ratio):
+            total = jnp.zeros((lay.width, lay.width), F32)
+            for group in range(one_columns // lay.ratio):
+                total = total + lay.read(dinv, row, group * lay.ratio + part, one_columns)
+            dinv_ref[:, lay.lanes(row * lay.ratio + part)] = total
     for slot, level_ref in enumerate(level_refs):
         stack_ref[slot] = level_ref[...]
-    root_count, level_count, one_columns, two_columns, root_total = counts
     prow_place, pcol_place = place_ref[0], place_ref[1]
     for index, column in lay.blocks(two_columns):
         node = seg_two[lay.column_id(column, pcol_place)]
@@ -114,21 +121,20 @@
             keep = two[node, root_row] * one[above, root_row]
             block = lay.read(lower_two, row, column, two_columns)
             second_ref[lay.lanes(row), lay.lanes(index)] = block * keep.astype(F32)
-    for row in range(level_count):
-        for part in range(lay.ratio):
-            total = jnp.zeros((lay.width, lay.width), F32)
-            for group in range(one_columns // lay.ratio):
-                total = total + lay.read(dinv, row, group * lay.ratio + part, one_columns)
-            dinv_ref[:, lay.lanes(row * lay.ratio + part)] = total
-
-
-def fill_panel(piece_refs, panel_ref):
+
+
+def start_fill(piece_refs, panel_ref, sem_ref):
     start = 0
     rows = panel_ref.shape[1]
-    for piece_ref in piece_refs:
+    copies = []
+    for index, piece_ref in enumerate(piece_refs):
         place, first = divmod(start, rows)
-        panel_ref[place, first : first + piece_ref.shape[0], :] = piece_ref[...]
+        lines = pl.ds(first, piece_ref.shape[0])
+        copy = pltpu.make_async_copy(piece_ref, panel_ref.at[place, lines, :], sem_ref.at[index])
+        copy.start()
+        copies.append(copy)
         start += piece_ref.shape[0]
+    return copies
 
 
 def panel_columns(lay, panel_ref, rows, source, flip, width):
@@ -156,17 +162,45 @@
     return source * 2 + lax.rem(row, 2)
 
 
-def solve_rows(lay, weights, source_of, place_ref, root_ref, slot_refs):
+def start_solve(lay, source_of, place_ref, root_ref, slot_refs, block_ref, held_ref, sem_ref):
     width = slot_refs[0].shape[0]
-    totals = {}
+    copies = []
     for slot, slot_ref in enumerate(slot_refs):
         source = source_of(lay, place_ref, slot)
-        root_part = panel_columns(lay, root_ref, slice(None), source, 0, width)
-        part = product(halves(root_part), halves(slot_ref[...]))
+        start = pl.multiple_of(lax.div(source, lay.pcol) * width, width)
+        columns = root_ref.at[lax.rem(source, lay.pcol), :, pl.ds(start, width)]
+        pair = (
+            pltpu.make_async_copy(columns, block_ref.at[slot], sem_ref.at[2 * slot]),
+            pltpu.make_async_copy(slot_ref, held_ref.at[slot], sem_ref.at[2 * slot + 1]),
+        )
+        for copy in pair:
+            copy.start()
+        copies.append(pair)
+    return copies
+
+
+def solve_rows(weights, copies, block_ref, held_ref):
+    totals = {}
+    for slot, pair in enumerate(copies):
+        for copy in pair:
+            copy.wait()
+        part = product(halves(block_ref[slot]), halves(held_ref[slot]))
         weight = weights[slot]
         totals[weight] = totals[weight] + part if weight in totals else part
     total = sum(part if weight == 1.0 else part * weight for weight, part in totals.items())
     return total.T
+
+
+def solve_scratch(slots, rows, width, columns):
+    return [
+        pltpu.VMEM((slots, rows, width), F32),
+        pltpu.VMEM((slots, width, columns), F32),
+        pltpu.SemaphoreType.DMA((2 * slots,)),
+    ]
+
+
+def panel_scratch(pieces, places, rows, columns):
+    return [pltpu.VMEM((places, rows, columns), F32), pltpu.SemaphoreType.DMA((pieces,))]
 
 
 def packed_diagonal(lay, place_ref, segment_ref, left, panel_ref, out_ref, groups, paired):
@@ -174,33 +208,37 @@
     depth = left[0].shape[1]
     pcol_place, flip = place_ref[1], place_ref[2]
     for place in range(lay.prow):
-        start = (place // lay.pcol) * groups * lay.width
+        part = place // lay.pcol
+        start = part * groups * lay.width
         columns = panel_ref[(place % lay.pcol) ^ flip, :depth, start : start + groups * lay.width]
         result = product(left, halves(columns))
         for index, column in lay.blocks(rows // lay.width):
             node = segment_ref[lay.column_id(column, pcol_place)]
             kept = jnp.zeros((lay.width, lay.width), F32)
             for group in range(groups):
-                part = result[lay.lanes(index), lay.lanes(group)]
                 same = segment_ref[group * lay.prow + place] == node
-                kept = kept + jnp.where(same, part, 0.0)
-            target = index
-            if paired and place >= lay.pcol:
-                target = (index + groups) % (2 * groups)
+                kept = kept + jnp.where(same, result[lay.lanes(index), lay.lanes(group)], 0.0)
+            target = (index + groups) % (2 * groups) if paired and part else index
             out_ref[place, lay.lanes(target), :] = kept
 
 
 def level_one_kernel(lay, weights, source_of, groups, pieces, place_ref, segment_ref, root_ref, *refs):
-    piece_refs, slot_refs = refs[:pieces], refs[pieces:-2]
-    out_ref, panel_ref = refs[-2:]
-    fill_panel(piece_refs, panel_ref)
-    solved = solve_rows(lay, weights, source_of, place_ref, root_ref, slot_refs)
+    piece_refs, slot_refs = refs[:pieces], refs[pieces : pieces + len(weights)]
+    out_ref, panel_ref, panel_sem, block_ref, held_ref, sem_ref = refs[pieces + len(weights) :]
+    copies = start_solve(lay, source_of, place_ref, root_ref, slot_refs, block_ref, held_ref, sem_ref)
+    fills = start_fill(piece_refs, panel_ref, panel_sem)
+    left = halves(solve_rows(weights, copies, block_ref, held_ref))
+    for copy in fills:
+        copy.wait()
     paired = source_of is paired_source
-    packed_diagonal(lay, place_ref, segment_ref, halves(solved), panel_ref, out_ref, groups, paired)
+    packed_diagonal(lay, place_ref, segment_ref, left, panel_ref, out_ref, groups, paired)
 
 
 def solve_two_kernel(lay, weights, source_of, place_ref, root_ref, *refs):
-    refs[-1][...] = solve_rows(lay, weights, source_of, place_ref, root_ref, refs[:-1])
+    slot_refs = refs[: len(weights)]
+    out_ref, block_ref, held_ref, sem_ref = refs[len(weights) :]
+    copies = start_solve(lay, source_of, place_ref, root_ref, slot_refs, block_ref, held_ref, sem_ref)
+    out_ref[...] = solve_rows(weights, copies, block_ref, held_ref)
 
 
 def keep_columns(lay, place_ref, seg_one, seg_two, parent, level_row, value):
@@ -216,14 +254,18 @@
     return level_refs[slot // half][slot % half]
 
 
-def level_two_kernel(lay, weight, groups, level_groups, pieces, place_ref, seg_one, seg_two, parent, solved_ref, *refs):
-    level_refs, piece_refs = refs[:2], refs[2 : 2 + pieces]
-    out_ref, panel_ref = refs[-2:]
-    fill_panel(piece_refs, panel_ref)
+def level_two_kernel(lay, paired, weight, groups, level_groups, place_ref, seg_one, seg_two, parent, *refs):
+    pieces = refs[-1].shape[0]
+    solved_ref, level_refs, piece_refs = refs[0], refs[1:3], refs[3 : 3 + pieces]
+    out_ref, panel_ref, panel_sem = refs[-3:]
+    fills = start_fill(piece_refs, panel_ref, panel_sem)
     width = lay.width
     depth = solved_ref.shape[1]
     columns = level_refs[0].shape[2]
-    total = jnp.zeros((level_groups * width, columns), F32)
+    solved = solved_ref[...]
+    for copy in fills:
+        copy.wait()
+    packed = jnp.zeros((level_groups * width, columns), F32)
     for slot in range(lay.prow):
         source = gathered_source(lay, place_ref, slot)
         place, part = lax.rem(source, lay.pcol) ^ place_ref[2], lax.div(source, lay.pcol)
@@ -232,23 +274,26 @@
             start = pl.multiple_of((group * lay.ratio + part) * width, width)
             dinv_parts.append(panel_ref[place, pl.ds(depth + width, width), pl.ds(start, width)])
         dinv_part = jnp.concatenate(dinv_parts, axis=0)
-        total = total + product(halves(dinv_part), halves(level_slot(level_refs, slot)))
+        packed = packed + product(halves(dinv_part), halves(level_slot(level_refs, slot)))
     extra = jnp.zeros((width, columns), F32)
     for group in range(level_groups):
         level_row = group * lay.prow + place_ref[0]
-        lines = total[lay.lanes(group), :]
+        lines = packed[lay.lanes(group), :]
         extra = extra + keep_columns(lay, place_ref, seg_one, seg_two, parent, level_row, lines)
-    left = jnp.concatenate([solved_ref[...], (extra * weight).T], axis=1)
-    packed_diagonal(lay, place_ref, seg_two, halves(left), panel_ref, out_ref, groups, weight != 1.0)
-
-
-def update_kernel(lay, groups, pieces, place_ref, seg_one, seg_two, parent, lower_ref, dinv_ref, *refs):
+    left = halves(jnp.concatenate([solved, (extra * weight).T], axis=1))
+    packed_diagonal(lay, place_ref, seg_two, left, panel_ref, out_ref, groups, paired)
+
+
+def update_kernel(lay, groups, place_ref, seg_one, seg_two, parent, lower_ref, dinv_ref, *refs):
+    pieces = refs[-1].shape[0]
     level_refs, piece_refs = refs[:2], refs[2 : 2 + pieces]
-    out_ref, bundle_ref, panel_ref = refs[-3:]
-    fill_panel(piece_refs, panel_ref)
+    out_ref, bundle_ref, panel_ref, panel_sem = refs[2 + pieces :]
+    fills = start_fill(piece_refs, panel_ref, panel_sem)
     width = lay.width
     rows = lower_ref.shape[0]
     total = jnp.zeros(lower_ref.shape, F32)
+    for copy in fills:
+        copy.wait()
     for slot in range(lay.prow):
         source = gathered_source(lay, place_ref, slot)
         panel_part = panel_columns(lay, panel_ref, slice(None), source, place_ref[2], groups * width)
@@ -265,22 +310,22 @@
     bundle_ref[rows + width :, :] = dinv_ref[...]
 
 
-def finish_kernel(lay, count, columns, paired, place_ref, segment_ref, diag_ref, dinv_ref, *refs):
+def finish_kernel(lay, count, place_ref, segment_ref, diag_ref, dinv_ref, *refs):
     turned_refs, out_ref = refs[:-1], refs[-1]
     prow_place, pcol_place = place_ref[0], place_ref[1]
+    columns = diag_ref.shape[0] // lay.width
     groups = columns // lay.ratio
     upper = lax.div(prow_place, lay.pcol)
     for index, column in lay.blocks(columns):
         start = index * lay.width
-        if paired:
+        if turned_refs:
             part = (index // groups) ^ upper
             start = pl.multiple_of((part * groups + index % groups) * lay.width, lay.width)
         block = diag_ref[pl.ds(start, lay.width), :].T
         for row in range(count):
             value = block
-            if paired:
-                lines = lay.lanes(row)
-                even, odd = (ref[lines, :] for ref in turned_refs)
+            if turned_refs:
+                even, odd = (ref[lay.lanes(row), :] for ref in turned_refs)
                 value = block + jnp.where(upper == index // groups, even, odd)
             same = (
                 segment_ref[row * lay.prow + prow_place]
@@ -417,23 +462,27 @@
 
     size = rows * one_columns * width
     bundle_rows = rows + 2 * width
+    pieces = len(first_pieces)
     second, bundle = vmem_call(
-        functools.partial(update_kernel, lay, groups_one, len(first_pieces)),
+        functools.partial(update_kernel, lay, groups_one),
         (out_shape(rows, two_columns * width), out_shape(bundle_rows, two_columns * width)),
         [place, seg_one, seg_two, parent_two],
-        [second_root, dinv_packed, *level_slots, *first_pieces],
-        [pltpu.VMEM((pcol_total, rows, one_columns * width), F32)],
+        [second_root, dinv_packed, *level_slots],
+        first_pieces,
+        panel_scratch(pieces, pcol_total, rows, one_columns * width),
         flops=6 * size * seg_one.shape[0] * width,
     )
     second_slots = start_slots(second)
     bundle, first_slots = tied(bundle, first_slots)
     bundle_started = start_panel(bundle)
     packed_one = vmem_call(
-        functools.partial(level_one_kernel, lay, weights, source_of, groups_one, len(first_pieces)),
+        functools.partial(level_one_kernel, lay, weights, source_of, groups_one, pieces),
         out_shape(prow_total, one_columns * width, width),
         [place, seg_one],
+        [],
         [root_panel, *first_pieces, *first_slots],
-        [pltpu.VMEM((pcol_total, rows, one_columns * width), F32)],
+        panel_scratch(pieces, pcol_total, rows, one_columns * width)
+        + solve_scratch(len(weights), rows, rows, one_columns * width),
         flops=6 * size * (root_total + seg_one.shape[0]) * width,
         after=[second],
     )
@@ -445,17 +494,21 @@
         functools.partial(solve_two_kernel, lay, weights, source_of),
         out_shape(two_columns * width, rows),
         [place],
+        [],
         [root_panel, *second_slots],
+        solve_scratch(len(weights), rows, rows, two_columns * width),
         flops=6 * size * root_total * width,
     )
     packed_two = vmem_call(
-        functools.partial(level_two_kernel, lay, weights[0], groups_two, level_count, len(bundle_pieces)),
+        functools.partial(level_two_kernel, lay, paired, weights[0], groups_two, level_count),
         out_shape(prow_total, two_columns * width, width),
         [place, seg_one, seg_two, parent_two],
-        [solved_two, *level_slots, *bundle_pieces],
-        [pltpu.VMEM((pcol_total, bundle_rows, two_columns * width), F32)],
+        [solved_two, *level_slots],
+        bundle_pieces,
+        panel_scratch(pieces, pcol_total, bundle_rows, two_columns * width),
         flops=6 * size * seg_two.shape[0] * width,
     )
+
     diag_two = lax.psum_scatter(packed_two, "prow", scatter_dimension=0, tiled=False)
 
     def partners(diag, groups):
@@ -474,7 +527,7 @@
     def finish(dinv, diag, segments, groups):
         count, columns = dinv.shape[0], dinv.shape[3]
         result = vmem_call(
-            functools.partial(finish_kernel, lay, count, columns, paired),
+            functools.partial(finish_kernel, lay, count),
             out_shape(count * width * columns, width),
             [place, segments],
             [diag, lines(dinv)] + (partners(diag, groups) if paired else []),

time: 253 us -> 254 us (level)
  Pallas kernels: 62.2 us -> 58 us
  waiting for transfers between devices: 127 us -> 131 us
    ppermute x8, waiting for transfers between devices: 9.5 us -> 14 us  [neighbour(): lax.ppermute(piece, 'pcol', [(place, place ^ flip) for place in range(pco...]
    pallas_call x9, Pallas kernels: 62.2 us -> 58 us  [vmem_call(): pl.pallas_call(body, out_shape=outs, in_specs=[pl.BlockSpec(memory_space=...]
  transfers between devices with their start and end apart: 29 -> 29, of which waited for: 14 -> 15; matrix products, arithmetic and copies ran while one was open for 1% -> 1% of each run, Pallas kernels for 22% -> 21%
where the time goes in v2:
time: 254 us; the launch traced here: 253 us
  waiting for transfers between devices  131 us (52%)
  Pallas kernels  58 us (23%)
  starting transfers between devices  43.3 us (17%)
  between operations  14 us (6%)
  local copies, waits for them, and re-layouts  6.58 us (3%)
    pallas_call x9, Pallas kernels, vmem_call(): pl.pallas_call(body, out_shape=outs, in_specs=[pl.BlockSpec(memory_space=...  58 us
    ppermute x7, waiting for transfers between devices, shift_rows(): lax.ppermute(piece, 'prow', [(2 * source + core, 2 * target + core) for s...  45.7 us
    reduce_scatter x1, waiting for transfers between devices, on_device(): lax.psum_scatter(packed_two, 'prow', scatter_dimension=0, tiled=False)  33.5 us
    all_gather x1, waiting for transfers between devices, on_device(): root_panel = lax.all_gather(root, 'pcol', axis=0, tiled=False)  24.9 us
    ppermute x7, starting transfers between devices, shift_rows(): lax.ppermute(piece, 'prow', [(2 * source + core, 2 * target + core) for s...  24.1 us
    ppermute x8, waiting for transfers between devices, neighbour(): lax.ppermute(piece, 'pcol', [(place, place ^ flip) for place in range(pco...  14 us
    ppermute x8, starting transfers between devices, neighbour(): lax.ppermute(piece, 'pcol', [(place, place ^ flip) for place in range(pco...  10.6 us
    ppermute x4, waiting for transfers between devices, partners(): turned.append(lax.ppermute(sent, BOTH, pairs))  8.29 us
  transfers between devices with their start and end apart: 29, of which 15 were waited for; matrix products, arithmetic and copies ran while one was open for 1% of the time, Pallas kernels for 21%

profile of v2, /device:TPU:4, one launch (start us, length us, event | category | flops | bytes accessed | tf_op | source)
XLA Modules:
  0.0 253.5 jit_solution(17653695772000584474)
XLA Ops:
  7.2 3.4 %shard_map.116 = f32[512,1024]{1,0:T(8,128)} custom-call(f32[4096,128]{1,0:T(8,128)} %bitcast.26), custom_call_target="tpu_custom_call" | custom-call | bytes 2097152 | tf_op jit(solution)/shard_map/pallas_call | solution.py:32
  10.7 0.6 pad_add_fusion.refs_0_.refs_1_
  11.3 3.0 %shard_map.113 = (f32[512,512]{1,0:T(8,128)}, f32[128,512]{1,0:T(8,128)}) custom-call(s32[3]{0:T(128)} %pad_add_fusion.refs_0_.refs_1_, s32[16]{0:T(128)} %refs_1_.10, s32[16]{0:T(128)} %refs_1_.11, s32[4]{0:T(128)} %refs_3_.7, s32[3,32]{1,0:T(4,128)} %refs_3_.5, s32[4,48]{1,0:T(4,128)} %refs_4_.3, f32[2048,128]{1,0:T(8,128)} %bitcast.29, f32[3072,128]{1,0:T(8,128)} %bitcast.24), custom_call_target="tpu_custom_call" | custom-call | bytes 2621440 | tf_op jit(solution)/shard_map/pallas_call | solution.py:32
  14.2 2.0 collective-permute-start.3
  16.2 1.6 collective-permute-start
  17.8 2.6 %collective-permute-start.1 = (f32[128,512]{1,0:T(8,128)}, f32[128,512]{1,0:T(8,128)S(1)}, u32[]{:S(2)}, u32[]{:S(2)}) collective-permute-start(f32[128,512]{1,0:T(8,128)} %get-tuple-element.35.refs_7_), channel_id=1, source_target_pairs={{0,16},{4,20},{8,24},{12,28},{16,0},{20,4},{24,8},{28,12},{1,17},{... | collective-permute-start | bytes 786440 | tf_op jit(solution)/shard_map/ppermute | solution.py:339
  20.4 1.3 collective-permute-start.2
  21.7 5.9 %collective-permute-done.refs_8_ = f32[128,512]{1,0:T(8,128)S(1)} collective-permute-done((f32[128,512]{1,0:T(8,128)}, f32[128,512]{1,0:T(8,128)S(1)}, u32[]{:S(2)}, u32[]{:S(2)}) %collective-permute-start) | collective-permute-done | bytes 262176 | tf_op jit(solution)/shard_map/ppermute | solution.py:339
  27.6 9.5 %collective-permute-done.1.refs_9_ = f32[128,512]{1,0:T(8,128)S(1)} collective-permute-done((f32[128,512]{1,0:T(8,128)}, f32[128,512]{1,0:T(8,128)S(1)}, u32[]{:S(2)}, u32[]{:S(2)}) %collective-permute-start.1) | collective-permute-done | bytes 262176 | tf_op jit(solution)/shard_map/ppermute | solution.py:339
  37.1 9.1 %collective-permute-start.9 = (f32[512,512]{1,0:T(8,128)}, f32[512,512]{1,0:T(8,128)S(1)}, u32[]{:S(2)}, u32[]{:S(2)}) collective-permute-start(f32[512,512]{1,0:T(8,128)} %get-tuple-element.55.refs_8_.refs_4_.refs_9_), channel_id=1, source_target_pairs={{16,8},{20,12},{0,24},{4,28},{17,9},{21,13},{1,25},{5,29},{18,10},... | collective-permute-start | bytes 3145736 | tf_op jit(solution)/shard_map/ppermute | solution.py:339
  46.3 3.4 %shard_map.114 = (f32[512,512]{1,0:T(8,128)}, f32[128,512]{1,0:T(8,128)}, f32[4,128,512]{2,1,0:T(8,128)}) custom-call(s32[3]{0:T(128)} %pad_add_fusion.refs_0_.refs_1_, s32[16]{0:T(128)} %refs_1_.11, s32[4]{0:T(128)} %refs_3_.7, s32[3,32]{1,0:T(4,128)} %refs_3_.5, s32[4,48]{1,0:T(4,128)} %refs_4_.3, f32[3072,128]{1,0:T(8,128)} %bitcast.25, ...), custom_call_target="tpu_custom_call" | custom-call | bytes 3145728 | tf_op jit(solution)/shard_map/pallas_call | solution.py:32
  50.1 6.5 %collective-permute-done.4.refs_10_.refs_6_ = f32[512,512]{1,0:T(8,128)S(1)} collective-permute-done((f32[512,512]{1,0:T(8,128)}, f32[512,512]{1,0:T(8,128)S(1)}, u32[]{:S(2)}, u32[]{:S(2)}) %collective-permute-start.4) | collective-permute-done | bytes 1048608 | tf_op jit(solution)/shard_map/ppermute | solution.py:360
  56.7 1.3 collective-permute-start.5
  58.1 3.0 %collective-permute-start.6 = (f32[256,512]{1,0:T(8,128)S(1)}, f32[256,512]{1,0:T(8,128)S(1)}, u32[]{:S(2)}, u32[]{:S(2)}) collective-permute-start(f32[256,512]{1,0:T(8,128)S(1)} %slice.49), channel_id=1, source_target_pairs={{0,2},{1,3},{2,0},{3,1},{4,6},{5,7},{6,4},{7,5},{8,10},{9,11},{10,... | collective-permute-start | bytes 1572872 | tf_op jit(solution)/shard_map/ppermute | solution.py:360
  61.1 9.0 %collective-permute-done.9.refs_11_ = f32[512,512]{1,0:T(8,128)S(1)} collective-permute-done((f32[512,512]{1,0:T(8,128)}, f32[512,512]{1,0:T(8,128)S(1)}, u32[]{:S(2)}, u32[]{:S(2)}) %collective-permute-start.9) | collective-permute-done | bytes 1048608 | tf_op jit(solution)/shard_map/ppermute | solution.py:339
  70.1 19.7 %collective-permute-done.8.refs_10_ = f32[512,512]{1,0:T(8,128)S(1)} collective-permute-done((f32[512,512]{1,0:T(8,128)S(1)}, f32[512,512]{1,0:T(8,128)S(1)}, u32[]{:S(2)}, u32[]{:S(2)}) %collective-permute-start.8) | collective-permute-done | bytes 1048608 | tf_op jit(solution)/shard_map/ppermute | solution.py:339
  89.9 0.9 copy-done.20
  90.8 9.2 %shard_map.115 = (f32[512,512]{1,0:T(8,128)}, f32[768,512]{1,0:T(8,128)}) custom-call(s32[3]{0:T(128)} %pad_add_fusion.refs_0_.refs_1_, s32[16]{0:T(128)} %refs_1_.10, s32[16]{0:T(128)} %refs_1_.11, s32[4]{0:T(128)} %refs_3_.7, f32[512,512]{1,0:T(8,128)} %get-tuple-element.40.refs_4_, f32[128,512]{1,0:T(8,128)} %get-tuple-element.41.refs_5_, ...), custom_call_target="tpu_custom_call" | custom-call | flops 3221225472 | bytes 7602176 | tf_op jit(solution)/shard_map/pallas_call | solution.py:32
  100.1 1.0 copy-done.15
  101.1 0.5 collective-permute-start.15
  101.6 1.5 collective-permute-start.16
  103.1 3.4 %collective-permute-start.13 = (f32[512,512]{1,0:T(8,128)}, f32[512,512]{1,0:T(8,128)}, u32[]{:S(2)}, u32[]{:S(2)}) collective-permute-start(f32[512,512]{1,0:T(8,128)} %get-tuple-element.63.refs_0_.refs_2_), channel_id=1, source_target_pairs={{8,0},{12,4},{24,8},{28,12},{0,16},{4,20},{16,24},{20,28},{9,1},{1... | collective-permute-start | bytes 3145736 | tf_op jit(solution)/shard_map/ppermute | solution.py:339
  106.5 5.6 %collective-permute-start.14 = (f32[512,512]{1,0:T(8,128)}, f32[512,512]{1,0:T(8,128)}, u32[]{:S(2)}, u32[]{:S(2)}) collective-permute-start(f32[512,512]{1,0:T(8,128)} %get-tuple-element.63.refs_0_.refs_2_), channel_id=1, source_target_pairs={{16,8},{20,12},{0,24},{4,28},{17,9},{21,13},{1,25},{5,29},{18,10},... | collective-permute-start | bytes 3145736 | tf_op jit(solution)/shard_map/ppermute | solution.py:339
  112.1 24.9 %all-gather.3.cloned.1.call-done = f32[2048,1024]{1,0:T(8,128)} async-done(((f32[512,1024]{1,0:T(8,128)}), f32[2048,1024]{1,0:T(8,128)}) %all-gather.3.cloned.1.call-update) | async-done | bytes 8388624 | tf_op jit(solution)/shard_map/all_gather | solution.py:412
  137.0 13.2 %shard_map.117 = f32[8,512,128]{2,1,0:T(8,128)} custom-call(f32[512,512]{1,0:T(8,128)} %get-tuple-element.63.refs_0_.refs_2_, s32[3]{0:T(128)} %pad_add_fusion.refs_0_.refs_1_, s32[16]{0:T(128)} %refs_1_.10, f32[4,512,1024]{2,1,0:T(8,128)} %bitcast.35, f32[512,512]{1,0:T(8,128)} %get-tuple-element.55.refs_8_.refs_4_.refs_9_, f32[512,512]{1,0:T(8,128)} %copy-done.6, ...), custom_call_target="tpu_custom_call" | custom-call | flops 9663676416 | bytes 18874368 | tf_op jit(solution)/shard_map/pallas_call | solution.py:32
  150.2 1.7 collective-permute-done.14.refs_4_
  151.8 2.3 collective-permute-done.15.refs_8_
  154.5 0.5 collective-permute-start.20
  155.2 0.6 collective-permute-start.22
  155.9 1.5 collective-permute-start.23
  157.4 1.5 collective-permute-done.20.refs_6_
  158.9 1.5 collective-permute-done.21.refs_7_
  160.4 1.1 copy-done.18
  161.5 9.0 %shard_map.119.refs_4_ = f32[512,512]{1,0:T(8,128)} custom-call(s32[3]{0:T(128)} %pad_add_fusion.refs_0_.refs_1_, f32[4,512,1024]{2,1,0:T(8,128)} %bitcast.36, f32[512,512]{1,0:T(8,128)} %get-tuple-element.63.refs_0_.refs_2_, f32[512,512]{1,0:T(8,128)} %collective-permute-done.13.refs_3_, f32[512,512]{1,0:T(8,128)} %collective-permute-done.14.refs_4_, ...), custom_call_target="tpu_custom_call" | custom-call | flops 6442450944 | bytes 14680064 | tf_op jit(solution)/shard_map/pallas_call | solution.py:32
  170.4 4.8 %collective-permute-done.22.refs_10_ = f32[384,512]{1,0:T(8,128)} collective-permute-done((f32[384,512]{1,0:T(8,128)S(1)}, f32[384,512]{1,0:T(8,128)}, u32[]{:S(2)}, u32[]{:S(2)}) %collective-permute-start.22) | collective-permute-done | bytes 786464 | tf_op jit(solution)/shard_map/ppermute | solution.py:360
  175.7 12.7 %shard_map.120 = f32[8,512,128]{2,1,0:T(8,128)} custom-call(s32[3]{0:T(128)} %pad_add_fusion.refs_0_.refs_1_, s32[16]{0:T(128)} %refs_1_.10, s32[16]{0:T(128)} %refs_1_.11, s32[4]{0:T(128)} %refs_3_.7, f32[512,512]{1,0:T(8,128)} %shard_map.119.refs_4_, f32[4,128,512]{2,1,0:T(8,128)} %get-tuple-element.44.refs_6_.refs_5_, f32[4,128,512]{2,1,0:T(8,128)} %copy-done.11, ...), custom_call_target="tpu_custom_call" | custom-call | flops 3221225472 | bytes 9437184 | tf_op jit(solution)/shard_map/pallas_call | solution.py:32
  188.4 1.5 reduce-scatter.3.cloned.1.call-done
  189.9 1.0 slice_bitcast_fusion.2
  190.9 2.9 %collective-permute-start.17 = (f32[256,128]{1,0:T(8,128)S(1)}, f32[256,128]{1,0:T(8,128)S(1)}, u32[]{:S(2)}, u32[]{:S(2)}) collective-permute-start(f32[256,128]{1,0:T(8,128)S(1)} %get-tuple-element.73), channel_id=1, source_target_pairs={{0,0},{1,4},{2,8},{3,12},{4,1},{5,5},{6,9},{7,13},{8,2},{9,6},{10,... | collective-permute-start | bytes 393224 | tf_op jit(solution)/shard_map/ppermute | solution.py:524
  193.8 2.4 collective-permute-start.18
  196.2 33.5 %reduce-scatter.5.cloned.1.call-done = f32[1,512,128]{2,1,0:T(8,128)} async-done(((f32[8,512,128]{2,1,0:T(8,128)}), f32[1,512,128]{2,1,0:T(8,128)}) %reduce-scatter.5.cloned.1.call-update) | async-done | bytes 262160 | tf_op jit(solution)/shard_map/reduce_scatter | solution.py:512
  229.7 1.0 slice_bitcast_fusion
  230.7 1.9 collective-permute-start.24
  233.0 0.6 copy-done.7
  233.7 2.1 shard_map.118
  235.9 8.3 %collective-permute-done.24.refs_4_ = f32[256,128]{1,0:T(8,128)S(1)} collective-permute-done((f32[256,128]{1,0:T(8,128)S(1)}, f32[256,128]{1,0:T(8,128)S(1)}, u32[]{:S(2)}, u32[]{:S(2)}) %collective-permute-start.24) | collective-permute-done | bytes 131104 | tf_op jit(solution)/shard_map/ppermute | solution.py:524
  244.2 0.7 copy-done.8
  244.8 2.1 shard_map.121
  (71 shorter events, 2.3 us)
Async XLA Ops:
  7.2 129.8 %all-gather.3.cloned.1.call-start = ((), (), s32[]{:S(2)}) async-start(), calls=%async_computation.4 | async-start | bytes 10485760 | tf_op jit(solution)/shard_map/all_gather | solution.py:412
  10.6 179.3 %reduce-scatter.3.cloned.1.call-start = ((), (), s32[]{:S(2)}) async-start(), calls=%async_computation.2 | async-start | bytes 2359296 | tf_op jit(solution)/shard_map/reduce_scatter | solution.py:491
  14.2 35.4 %copy-start.12 = (f32[512,512]{1,0:T(8,128)S(1)}, f32[512,512]{1,0:T(8,128)}, u32[]{:S(2)}) copy-start(f32[512,512]{1,0:T(8,128)} %get-tuple-element.55.refs_8_.refs_4_.refs_9_) | copy-start | bytes 3145732
  14.2 42.4 %collective-permute-start.4 = (f32[512,512]{1,0:T(8,128)}, f32[512,512]{1,0:T(8,128)S(1)}, u32[]{:S(2)}, u32[]{:S(2)}) collective-permute-start(f32[512,512]{1,0:T(8,128)} %get-tuple-element.55.refs_8_.refs_4_.refs_9_), channel_id=1, source_target_pairs={{0,2},{1,3},{2,0},{3,1},{4,6},{5,7},{6,4},{7,5},{8,10},{9,11},{10,... | collective-permute-start | bytes 3145736 | tf_op jit(solution)/shard_map/ppermute | solution.py:360
  14.2 43.8 %collective-permute-start.3 = (f32[512,512]{1,0:T(8,128)}, f32[512,512]{1,0:T(8,128)S(1)}, u32[]{:S(2)}, u32[]{:S(2)}) collective-permute-start(f32[512,512]{1,0:T(8,128)} %get-tuple-element.55.refs_8_.refs_4_.refs_9_), channel_id=1, source_target_pairs={{0,1},{1,0},{2,3},{3,2},{4,5},{5,4},{6,7},{7,6},{8,9},{9,8},{10,11... | collective-permute-start | bytes 3145736 | tf_op jit(solution)/shard_map/ppermute | solution.py:360
  16.2 11.4 %collective-permute-start = (f32[128,512]{1,0:T(8,128)}, f32[128,512]{1,0:T(8,128)S(1)}, u32[]{:S(2)}, u32[]{:S(2)}) collective-permute-start(f32[128,512]{1,0:T(8,128)} %get-tuple-element.35.refs_7_), channel_id=1, source_target_pairs={{0,8},{4,12},{8,16},{12,20},{16,24},{20,28},{24,0},{28,4},{1,9},{5... | collective-permute-start | bytes 786440 | tf_op jit(solution)/shard_map/ppermute | solution.py:339
  17.8 19.3 %collective-permute-start.1 = (f32[128,512]{1,0:T(8,128)}, f32[128,512]{1,0:T(8,128)S(1)}, u32[]{:S(2)}, u32[]{:S(2)}) collective-permute-start(f32[128,512]{1,0:T(8,128)} %get-tuple-element.35.refs_7_), channel_id=1, source_target_pairs={{0,16},{4,20},{8,24},{12,28},{16,0},{20,4},{24,8},{28,12},{1,17},{... | collective-permute-start | bytes 786440 | tf_op jit(solution)/shard_map/ppermute | solution.py:339
  20.4 16.8 %collective-permute-start.2 = (f32[128,512]{1,0:T(8,128)}, f32[128,512]{1,0:T(8,128)S(1)}, u32[]{:S(2)}, u32[]{:S(2)}) collective-permute-start(f32[128,512]{1,0:T(8,128)} %get-tuple-element.35.refs_7_), channel_id=1, source_target_pairs={{0,24},{4,28},{8,0},{12,4},{16,8},{20,12},{24,16},{28,20},{1,25},{... | collective-permute-start | bytes 786440 | tf_op jit(solution)/shard_map/ppermute | solution.py:339
  27.6 18.6 %copy-start.2 = (f32[128,512]{1,0:T(8,128)}, f32[128,512]{1,0:T(8,128)S(1)}, u32[]{:S(2)}) copy-start(f32[128,512]{1,0:T(8,128)S(1)} %collective-permute-done.refs_8_) | copy-start | bytes 786436
  37.1 9.1 %copy-start.3 = (f32[128,512]{1,0:T(8,128)}, f32[128,512]{1,0:T(8,128)S(1)}, u32[]{:S(2)}) copy-start(f32[128,512]{1,0:T(8,128)S(1)} %collective-permute-done.1.refs_9_) | copy-start | bytes 786436
  37.1 9.1 %copy-start.4 = (f32[128,512]{1,0:T(8,128)}, f32[128,512]{1,0:T(8,128)S(1)}, u32[]{:S(2)}) copy-start(f32[128,512]{1,0:T(8,128)S(1)} %collective-permute-done.2.refs_10_) | copy-start | bytes 786436
  37.1 32.9 %collective-permute-start.9 = (f32[512,512]{1,0:T(8,128)}, f32[512,512]{1,0:T(8,128)S(1)}, u32[]{:S(2)}, u32[]{:S(2)}) collective-permute-start(f32[512,512]{1,0:T(8,128)} %get-tuple-element.55.refs_8_.refs_4_.refs_9_), channel_id=1, source_target_pairs={{16,8},{20,12},{0,24},{4,28},{17,9},{21,13},{1,25},{5,29},{18,10},... | collective-permute-start | bytes 3145736 | tf_op jit(solution)/shard_map/ppermute | solution.py:339
  49.6 20.4 %collective-permute-start.7 = (f32[4,128,512]{2,1,0:T(8,128)}, f32[4,128,512]{2,1,0:T(8,128)S(1)}, u32[]{:S(2)}, u32[]{:S(2)}) collective-permute-start(f32[4,128,512]{2,1,0:T(8,128)} %get-tuple-element.44.refs_6_.refs_5_), channel_id=1, source_target_pairs={{0,4},{4,0},{8,12},{12,8},{16,20},{20,16},{24,28},{28,24},{1,5},{5... | collective-permute-start | bytes 3145736 | tf_op jit(solution)/shard_map/ppermute | solution.py:353
  49.7 40.1 %collective-permute-start.8 = (f32[512,512]{1,0:T(8,128)S(1)}, f32[512,512]{1,0:T(8,128)S(1)}, u32[]{:S(2)}, u32[]{:S(2)}) collective-permute-start(f32[512,512]{1,0:T(8,128)S(1)} %copy-done.12), channel_id=1, source_target_pairs={{8,0},{12,4},{24,8},{28,12},{0,16},{4,20},{16,24},{20,28},{9,1},{1... | collective-permute-start | bytes 3145736 | tf_op jit(solution)/shard_map/ppermute | solution.py:339
  56.6 34.2 %copy-start.5 = (f32[512,512]{1,0:T(8,128)}, f32[512,512]{1,0:T(8,128)S(1)}, u32[]{:S(2)}) copy-start(f32[512,512]{1,0:T(8,128)S(1)} %collective-permute-done.4.refs_10_.refs_6_) | copy-start | bytes 3145732
  56.7 33.1 %collective-permute-start.5 = (f32[256,512]{1,0:T(8,128)S(1)}, f32[256,512]{1,0:T(8,128)S(1)}, u32[]{:S(2)}, u32[]{:S(2)}) collective-permute-start(f32[256,512]{1,0:T(8,128)S(1)} %slice.48), channel_id=1, source_target_pairs={{0,1},{1,0},{2,3},{3,2},{4,5},{5,4},{6,7},{7,6},{8,9},{9,8},{10,11... | collective-permute-start | bytes 1572872 | tf_op jit(solution)/shard_map/ppermute | solution.py:360
  58.0 32.8 %copy-start.6 = (f32[512,512]{1,0:T(8,128)}, f32[512,512]{1,0:T(8,128)S(1)}, u32[]{:S(2)}) copy-start(f32[512,512]{1,0:T(8,128)S(1)} %collective-permute-done.3.refs_9_.refs_5_) | copy-start | bytes 3145732
  58.1 31.7 %collective-permute-start.6 = (f32[256,512]{1,0:T(8,128)S(1)}, f32[256,512]{1,0:T(8,128)S(1)}, u32[]{:S(2)}, u32[]{:S(2)}) collective-permute-start(f32[256,512]{1,0:T(8,128)S(1)} %slice.49), channel_id=1, source_target_pairs={{0,2},{1,3},{2,0},{3,1},{4,6},{5,7},{6,4},{7,5},{8,10},{9,11},{10,... | collective-permute-start | bytes 1572872 | tf_op jit(solution)/shard_map/ppermute | solution.py:360
  70.1 30.0 %copy-start.13 = (f32[512,512]{1,0:T(8,128)}, f32[512,512]{1,0:T(8,128)S(1)}, u32[]{:S(2)}) copy-start(f32[512,512]{1,0:T(8,128)S(1)} %collective-permute-done.9.refs_11_) | copy-start | bytes 3145732
  70.1 29.9 %collective-permute-start.12 = (f32[512,512]{1,0:T(8,128)S(1)}, f32[512,512]{1,0:T(8,128)S(1)}, u32[]{:S(2)}, u32[]{:S(2)}) collective-permute-start(f32[512,512]{1,0:T(8,128)S(1)} %collective-permute-done.9.refs_11_), channel_id=1, source_target_pairs={{0,4},{4,0},{8,12},{12,8},{16,20},{20,16},{24,28},{28,24},{1,5},{5... | collective-permute-start | bytes 3145736 | tf_op jit(solution)/shard_map/ppermute | solution.py:353
  70.1 20.7 %copy-start.11 = (f32[4,128,512]{2,1,0:T(8,128)}, f32[4,128,512]{2,1,0:T(8,128)S(1)}, u32[]{:S(2)}) copy-start(f32[4,128,512]{2,1,0:T(8,128)S(1)} %collective-permute-done.7.refs_7_.refs_6_) | copy-start | bytes 3145732
  89.8 10.2 %copy-start.14 = (f32[512,512]{1,0:T(8,128)}, f32[512,512]{1,0:T(8,128)S(1)}, u32[]{:S(2)}) copy-start(f32[512,512]{1,0:T(8,128)S(1)} %collective-permute-done.8.refs_10_) | copy-start | bytes 3145732
  89.8 1.1 copy-start.19
  89.8 1.0 copy-start.20
  89.8 10.2 %collective-permute-start.10 = (f32[512,512]{1,0:T(8,128)S(1)}, f32[512,512]{1,0:T(8,128)}, u32[]{:S(2)}, u32[]{:S(2)}) collective-permute-start(f32[512,512]{1,0:T(8,128)S(1)} %copy-done.12), channel_id=1, source_target_pairs={{0,4},{4,0},{8,12},{12,8},{16,20},{20,16},{24,28},{28,24},{1,5},{5... | collective-permute-start | bytes 3145736 | tf_op jit(solution)/shard_map/ppermute | solution.py:353
  90.8 9.2 %collective-permute-start.11 = (f32[512,512]{1,0:T(8,128)S(1)}, f32[512,512]{1,0:T(8,128)}, u32[]{:S(2)}, u32[]{:S(2)}) collective-permute-start(f32[512,512]{1,0:T(8,128)S(1)} %collective-permute-done.8.refs_10_), channel_id=1, source_target_pairs={{0,4},{4,0},{8,12},{12,8},{16,20},{20,16},{24,28},{28,24},{1,5},{5... | collective-permute-start | bytes 3145736 | tf_op jit(solution)/shard_map/ppermute | solution.py:353
  100.0 1.1 copy-start.15
  101.1 53.1 %collective-permute-start.15 = (f32[768,512]{1,0:T(8,128)}, f32[768,512]{1,0:T(8,128)S(1)}, u32[]{:S(2)}, u32[]{:S(2)}) collective-permute-start(f32[768,512]{1,0:T(8,128)} %get-tuple-element.61.refs_7_), channel_id=1, source_target_pairs={{0,1},{1,0},{2,3},{3,2},{4,5},{5,4},{6,7},{7,6},{8,9},{9,8},{10,11... | collective-permute-start | bytes 4718600 | tf_op jit(solution)/shard_map/ppermute | solution.py:360
  101.6 52.6 %collective-permute-start.16 = (f32[768,512]{1,0:T(8,128)}, f32[768,512]{1,0:T(8,128)S(1)}, u32[]{:S(2)}, u32[]{:S(2)}) collective-permute-start(f32[768,512]{1,0:T(8,128)} %get-tuple-element.61.refs_7_), channel_id=1, source_target_pairs={{0,2},{1,3},{2,0},{3,1},{4,6},{5,7},{6,4},{7,5},{8,10},{9,11},{10,... | collective-permute-start | bytes 4718600 | tf_op jit(solution)/shard_map/ppermute | solution.py:360
  103.1 47.0 %collective-permute-start.13 = (f32[512,512]{1,0:T(8,128)}, f32[512,512]{1,0:T(8,128)}, u32[]{:S(2)}, u32[]{:S(2)}) collective-permute-start(f32[512,512]{1,0:T(8,128)} %get-tuple-element.63.refs_0_.refs_2_), channel_id=1, source_target_pairs={{8,0},{12,4},{24,8},{28,12},{0,16},{4,20},{16,24},{20,28},{9,1},{1... | collective-permute-start | bytes 3145736 | tf_op jit(solution)/shard_map/ppermute | solution.py:339
  106.5 45.3 %collective-permute-start.14 = (f32[512,512]{1,0:T(8,128)}, f32[512,512]{1,0:T(8,128)}, u32[]{:S(2)}, u32[]{:S(2)}) collective-permute-start(f32[512,512]{1,0:T(8,128)} %get-tuple-element.63.refs_0_.refs_2_), channel_id=1, source_target_pairs={{16,8},{20,12},{0,24},{4,28},{17,9},{21,13},{1,25},{5,29},{18,10},... | collective-permute-start | bytes 3145736 | tf_op jit(solution)/shard_map/ppermute | solution.py:339
  154.2 1.7 copy-start
  154.2 1.7 copy-start.1
  154.2 75.5 %reduce-scatter.5.cloned.1.call-start = ((), (), s32[]{:S(2)}) async-start(), calls=%async_computation.3 | async-start | bytes 2359296 | tf_op jit(solution)/shard_map/reduce_scatter | solution.py:512
  154.5 2.9 %collective-permute-start.19 = (f32[512,512]{1,0:T(8,128)}, f32[512,512]{1,0:T(8,128)S(1)}, u32[]{:S(2)}, u32[]{:S(2)}) collective-permute-start(f32[512,512]{1,0:T(8,128)} %get-tuple-element.63.refs_0_.refs_2_), channel_id=1, source_target_pairs={{0,4},{4,0},{8,12},{12,8},{16,20},{20,16},{24,28},{28,24},{1,5},{5... | collective-permute-start | bytes 3145736 | tf_op jit(solution)/shard_map/ppermute | solution.py:353
  154.5 4.4 %collective-permute-start.20 = (f32[512,512]{1,0:T(8,128)}, f32[512,512]{1,0:T(8,128)S(1)}, u32[]{:S(2)}, u32[]{:S(2)}) collective-permute-start(f32[512,512]{1,0:T(8,128)} %collective-permute-done.13.refs_3_), channel_id=1, source_target_pairs={{0,4},{4,0},{8,12},{12,8},{16,20},{20,16},{24,28},{28,24},{1,5},{5... | collective-permute-start | bytes 3145736 | tf_op jit(solution)/shard_map/ppermute | solution.py:353
  155.0 5.4 %collective-permute-start.21 = (f32[512,512]{1,0:T(8,128)}, f32[512,512]{1,0:T(8,128)S(1)}, u32[]{:S(2)}, u32[]{:S(2)}) collective-permute-start(f32[512,512]{1,0:T(8,128)} %collective-permute-done.14.refs_4_), channel_id=1, source_target_pairs={{0,4},{4,0},{8,12},{12,8},{16,20},{20,16},{24,28},{28,24},{1,5},{5... | collective-permute-start | bytes 3145736 | tf_op jit(solution)/shard_map/ppermute | solution.py:353
  155.2 20.1 %collective-permute-start.22 = (f32[384,512]{1,0:T(8,128)S(1)}, f32[384,512]{1,0:T(8,128)}, u32[]{:S(2)}, u32[]{:S(2)}) collective-permute-start(f32[384,512]{1,0:T(8,128)S(1)} %slice.42), channel_id=1, source_target_pairs={{0,1},{1,0},{2,3},{3,2},{4,5},{5,4},{6,7},{7,6},{8,9},{9,8},{10,11... | collective-permute-start | bytes 2359304 | tf_op jit(solution)/shard_map/ppermute | solution.py:360
  155.9 19.8 %collective-permute-start.23 = (f32[384,512]{1,0:T(8,128)S(1)}, f32[384,512]{1,0:T(8,128)}, u32[]{:S(2)}, u32[]{:S(2)}) collective-permute-start(f32[384,512]{1,0:T(8,128)S(1)} %slice.43), channel_id=1, source_target_pairs={{0,2},{1,3},{2,0},{3,1},{4,6},{5,7},{6,4},{7,5},{8,10},{9,11},{10,... | collective-permute-start | bytes 2359304 | tf_op jit(solution)/shard_map/ppermute | solution.py:360
  157.4 3.0 %copy-start.16 = (f32[512,512]{1,0:T(8,128)}, f32[512,512]{1,0:T(8,128)S(1)}, u32[]{:S(2)}) copy-start(f32[512,512]{1,0:T(8,128)S(1)} %collective-permute-done.19.refs_5_) | copy-start | bytes 3145732
  158.9 1.5 copy-start.17
  160.4 1.1 copy-start.18
  190.9 42.1 %collective-permute-start.17 = (f32[256,128]{1,0:T(8,128)S(1)}, f32[256,128]{1,0:T(8,128)S(1)}, u32[]{:S(2)}, u32[]{:S(2)}) collective-permute-start(f32[256,128]{1,0:T(8,128)S(1)} %get-tuple-element.73), channel_id=1, source_target_pairs={{0,0},{1,4},{2,8},{3,12},{4,1},{5,5},{6,9},{7,13},{8,2},{9,6},{10,... | collective-permute-start | bytes 393224 | tf_op jit(solution)/shard_map/ppermute | solution.py:524
  193.8 39.2 %collective-permute-start.18 = (f32[256,128]{1,0:T(8,128)S(1)}, f32[256,128]{1,0:T(8,128)S(1)}, u32[]{:S(2)}, u32[]{:S(2)}) collective-permute-start(f32[256,128]{1,0:T(8,128)S(1)} %get-tuple-element.72), channel_id=1, source_target_pairs={{0,16},{1,20},{2,24},{3,28},{4,17},{5,21},{6,25},{7,29},{8,18},{9,... | collective-permute-start | bytes 393224 | tf_op jit(solution)/shard_map/ppermute | solution.py:524
  230.7 13.4 %collective-permute-start.24 = (f32[256,128]{1,0:T(8,128)S(1)}, f32[256,128]{1,0:T(8,128)S(1)}, u32[]{:S(2)}, u32[]{:S(2)}) collective-permute-start(f32[256,128]{1,0:T(8,128)S(1)} %get-tuple-element.71), channel_id=1, source_target_pairs={{0,0},{1,4},{2,8},{3,12},{4,1},{5,5},{6,9},{7,13},{8,2},{9,6},{10,... | collective-permute-start | bytes 393224 | tf_op jit(solution)/shard_map/ppermute | solution.py:524
  232.6 11.5 %collective-permute-start.25 = (f32[256,128]{1,0:T(8,128)S(1)}, f32[256,128]{1,0:T(8,128)S(1)}, u32[]{:S(2)}, u32[]{:S(2)}) collective-permute-start(f32[256,128]{1,0:T(8,128)S(1)} %get-tuple-element.70), channel_id=1, source_target_pairs={{0,16},{1,20},{2,24},{3,28},{4,17},{5,21},{6,25},{7,29},{8,18},{9,... | collective-permute-start | bytes 393224 | tf_op jit(solution)/shard_map/ppermute | solution.py:524
  233.0 0.7 copy-start.9
  244.2 0.7 copy-start.10
  (2 other events, 1.3 us)
Sparse Core Ops, SparseCore 0:
  10.7 126.1 all-gather.2
  154.3 35.5 reduce-scatter.2
  192.2 37.4 reduce-scatter.4

commit v3 on v2

--- a/solution.py
+++ b/solution.py
@@ -407,6 +407,7 @@
         out_shape(rows, root_columns * width),
         [],
         [lines(root_inverse)],
+        after=[first],
     )
 
     root_panel = lax.all_gather(root, "pcol", axis=0, tiled=False)

time: 254 us -> 258 us (1.016)
    all_gather x1, waiting for transfers between devices: 24.9 us -> 30.8 us  [on_device(): root_panel = lax.all_gather(root, 'pcol', axis=0, tiled=False)]
    ppermute x8, waiting for transfers between devices: 14 us -> 10 us  [neighbour(): lax.ppermute(piece, 'pcol', [(place, place ^ flip) for place in range(pco...]
    unnamed x42 -> x44, local copies, waits for them, and re-layouts: 4.44 us -> 5.59 us
  transfers between devices with their start and end apart: 29 -> 29, of which waited for: 15 -> 14; matrix products, arithmetic and copies ran while one was open for 1% -> 1% of each run, Pallas kernels for 21% -> 19%
where the time goes in v3:
time: 258 us; the launch traced here: 257 us
  waiting for transfers between devices  133 us (52%)
  Pallas kernels  58.2 us (23%)
  starting transfers between devices  43.2 us (17%)
  between operations  14 us (5%)
  local copies, waits for them, and re-layouts  7.73 us (3%)
    pallas_call x9, Pallas kernels, vmem_call(): pl.pallas_call(body, out_shape=outs, in_specs=[pl.BlockSpec(memory_space=...  58.2 us
    ppermute x7, waiting for transfers between devices, shift_rows(): lax.ppermute(piece, 'prow', [(2 * source + core, 2 * target + core) for s...  46.4 us
    reduce_scatter x1, waiting for transfers between devices, on_device(): lax.psum_scatter(packed_two, 'prow', scatter_dimension=0, tiled=False)  33.4 us
    all_gather x1, waiting for transfers between devices, on_device(): root_panel = lax.all_gather(root, 'pcol', axis=0, tiled=False)  30.8 us
    ppermute x7, starting transfers between devices, shift_rows(): lax.ppermute(piece, 'prow', [(2 * source + core, 2 * target + core) for s...  23.9 us
    ppermute x8, starting transfers between devices, neighbour(): lax.ppermute(piece, 'pcol', [(place, place ^ flip) for place in range(pco...  10.4 us
    ppermute x8, waiting for transfers between devices, neighbour(): lax.ppermute(piece, 'pcol', [(place, place ^ flip) for place in range(pco...  10 us
    ppermute x4, waiting for transfers between devices, partners(): turned.append(lax.ppermute(sent, BOTH, pairs))  8.16 us
  transfers between devices with their start and end apart: 29, of which 14 were waited for; matrix products, arithmetic and copies ran while one was open for 1% of the time, Pallas kernels for 19%

profile of v3, /device:TPU:4, one launch (start us, length us, event | category | flops | bytes accessed | tf_op | source)
XLA Modules:
  0.0 257.1 jit_solution(17853835934127147538)
XLA Ops:
  7.2 0.7 pad_add_fusion.refs_0_.refs_1_
  7.9 3.0 %shard_map.113 = (f32[512,512]{1,0:T(8,128)}, f32[128,512]{1,0:T(8,128)}) custom-call(s32[3]{0:T(128)} %pad_add_fusion.refs_0_.refs_1_, s32[16]{0:T(128)} %refs_1_.10, s32[16]{0:T(128)} %refs_1_.11, s32[4]{0:T(128)} %refs_3_.7, s32[3,32]{1,0:T(4,128)} %refs_3_.5, s32[4,48]{1,0:T(4,128)} %refs_4_.3, f32[2048,128]{1,0:T(8,128)} %bitcast.29, f32[3072,128]{1,0:T(8,128)} %bitcast.24), custom_call_target="tpu_custom_call" | custom-call | bytes 2621440 | tf_op jit(solution)/shard_map/pallas_call | solution.py:32
  10.8 3.4 %shard_map.116 = f32[512,1024]{1,0:T(8,128)} custom-call(f32[512,512]{1,0:T(8,128)} %get-tuple-element.55.refs_8_.refs_0_.refs_4_.refs_9_, f32[4096,128]{1,0:T(8,128)} %bitcast.26), custom_call_target="tpu_custom_call" | custom-call | bytes 2097152 | tf_op jit(solution)/shard_map/pallas_call | solution.py:32
  14.3 1.1 copy-done
  15.5 2.0 collective-permute-start.3
  17.5 1.6 collective-permute-start
  19.0 2.6 %collective-permute-start.1 = (f32[128,512]{1,0:T(8,128)S(1)}, f32[128,512]{1,0:T(8,128)S(1)}, u32[]{:S(2)}, u32[]{:S(2)}) collective-permute-start(f32[128,512]{1,0:T(8,128)S(1)} %copy-done.3), channel_id=1, source_target_pairs={{0,16},{4,20},{8,24},{12,28},{16,0},{20,4},{24,8},{28,12},{1,17},{... | collective-permute-start | bytes 786440 | tf_op jit(solution)/shard_map/ppermute | solution.py:339
  21.6 1.3 collective-permute-start.2
  23.0 5.7 %collective-permute-done.refs_8_ = f32[128,512]{1,0:T(8,128)S(1)} collective-permute-done((f32[128,512]{1,0:T(8,128)S(1)}, f32[128,512]{1,0:T(8,128)S(1)}, u32[]{:S(2)}, u32[]{:S(2)}) %collective-permute-start) | collective-permute-done | bytes 262176 | tf_op jit(solution)/shard_map/ppermute | solution.py:339
  28.6 9.5 %collective-permute-done.1.refs_9_ = f32[128,512]{1,0:T(8,128)S(1)} collective-permute-done((f32[128,512]{1,0:T(8,128)S(1)}, f32[128,512]{1,0:T(8,128)S(1)}, u32[]{:S(2)}, u32[]{:S(2)}) %collective-permute-start.1) | collective-permute-done | bytes 262176 | tf_op jit(solution)/shard_map/ppermute | solution.py:339
  38.2 9.1 %collective-permute-start.9 = (f32[512,512]{1,0:T(8,128)S(1)}, f32[512,512]{1,0:T(8,128)S(1)}, u32[]{:S(2)}, u32[]{:S(2)}) collective-permute-start(f32[512,512]{1,0:T(8,128)S(1)} %copy-done), channel_id=1, source_target_pairs={{16,8},{20,12},{0,24},{4,28},{17,9},{21,13},{1,25},{5,29},{18,10},... | collective-permute-start | bytes 3145736 | tf_op jit(solution)/shard_map/ppermute | solution.py:339
  47.3 3.4 %shard_map.114 = (f32[512,512]{1,0:T(8,128)}, f32[128,512]{1,0:T(8,128)}, f32[4,128,512]{2,1,0:T(8,128)}) custom-call(s32[3]{0:T(128)} %pad_add_fusion.refs_0_.refs_1_, s32[16]{0:T(128)} %refs_1_.11, s32[4]{0:T(128)} %refs_3_.7, s32[3,32]{1,0:T(4,128)} %refs_3_.5, s32[4,48]{1,0:T(4,128)} %refs_4_.3, f32[3072,128]{1,0:T(8,128)} %bitcast.25, ...), custom_call_target="tpu_custom_call" | custom-call | bytes 3145728 | tf_op jit(solution)/shard_map/pallas_call | solution.py:32
  51.2 3.9 %collective-permute-done.4.refs_10_.refs_6_ = f32[512,512]{1,0:T(8,128)S(1)} collective-permute-done((f32[512,512]{1,0:T(8,128)S(1)}, f32[512,512]{1,0:T(8,128)S(1)}, u32[]{:S(2)}, u32[]{:S(2)}) %collective-permute-start.4) | collective-permute-done | bytes 1048608 | tf_op jit(solution)/shard_map/ppermute | solution.py:360
  55.1 1.3 collective-permute-start.5
  56.5 2.9 %collective-permute-start.6 = (f32[256,512]{1,0:T(8,128)S(1)}, f32[256,512]{1,0:T(8,128)S(1)}, u32[]{:S(2)}, u32[]{:S(2)}) collective-permute-start(f32[256,512]{1,0:T(8,128)S(1)} %slice.49), channel_id=1, source_target_pairs={{0,2},{1,3},{2,0},{3,1},{4,6},{5,7},{6,4},{7,5},{8,10},{9,11},{10,... | collective-permute-start | bytes 1572872 | tf_op jit(solution)/shard_map/ppermute | solution.py:360
  59.3 11.4 %collective-permute-done.9.refs_11_ = f32[512,512]{1,0:T(8,128)S(1)} collective-permute-done((f32[512,512]{1,0:T(8,128)S(1)}, f32[512,512]{1,0:T(8,128)S(1)}, u32[]{:S(2)}, u32[]{:S(2)}) %collective-permute-start.9) | collective-permute-done | bytes 1048608 | tf_op jit(solution)/shard_map/ppermute | solution.py:339
  70.8 19.8 %collective-permute-done.8.refs_10_ = f32[512,512]{1,0:T(8,128)S(1)} collective-permute-done((f32[512,512]{1,0:T(8,128)S(1)}, f32[512,512]{1,0:T(8,128)S(1)}, u32[]{:S(2)}, u32[]{:S(2)}) %collective-permute-start.8) | collective-permute-done | bytes 1048608 | tf_op jit(solution)/shard_map/ppermute | solution.py:339
  90.7 0.7 copy-done.20
  91.6 9.2 %shard_map.115 = (f32[512,512]{1,0:T(8,128)}, f32[768,512]{1,0:T(8,128)}) custom-call(s32[3]{0:T(128)} %pad_add_fusion.refs_0_.refs_1_, s32[16]{0:T(128)} %refs_1_.10, s32[16]{0:T(128)} %refs_1_.11, s32[4]{0:T(128)} %refs_3_.7, f32[512,512]{1,0:T(8,128)} %get-tuple-element.40.refs_4_, f32[128,512]{1,0:T(8,128)} %get-tuple-element.41.refs_5_, ...), custom_call_target="tpu_custom_call" | custom-call | flops 3221225472 | bytes 7602176 | tf_op jit(solution)/shard_map/pallas_call | solution.py:32
  100.9 1.0 copy-done.16
  101.9 0.5 collective-permute-start.15
  102.4 1.5 collective-permute-start.16
  103.9 3.4 %collective-permute-start.13 = (f32[512,512]{1,0:T(8,128)}, f32[512,512]{1,0:T(8,128)}, u32[]{:S(2)}, u32[]{:S(2)}) collective-permute-start(f32[512,512]{1,0:T(8,128)} %get-tuple-element.63.refs_0_.refs_2_), channel_id=1, source_target_pairs={{8,0},{12,4},{24,8},{28,12},{0,16},{4,20},{16,24},{20,28},{9,1},{1... | collective-permute-start | bytes 3145736 | tf_op jit(solution)/shard_map/ppermute | solution.py:339
  107.4 5.4 %collective-permute-start.14 = (f32[512,512]{1,0:T(8,128)}, f32[512,512]{1,0:T(8,128)}, u32[]{:S(2)}, u32[]{:S(2)}) collective-permute-start(f32[512,512]{1,0:T(8,128)} %get-tuple-element.63.refs_0_.refs_2_), channel_id=1, source_target_pairs={{16,8},{20,12},{0,24},{4,28},{17,9},{21,13},{1,25},{5,29},{18,10},... | collective-permute-start | bytes 3145736 | tf_op jit(solution)/shard_map/ppermute | solution.py:339
  112.8 30.8 %all-gather.3.cloned.1.call-done = f32[2048,1024]{1,0:T(8,128)} async-done(((f32[512,1024]{1,0:T(8,128)}), f32[2048,1024]{1,0:T(8,128)}) %all-gather.3.cloned.1.call-update) | async-done | bytes 8388624 | tf_op jit(solution)/shard_map/all_gather | solution.py:413
  143.6 13.3 %shard_map.117 = f32[8,512,128]{2,1,0:T(8,128)} custom-call(f32[512,512]{1,0:T(8,128)} %get-tuple-element.63.refs_0_.refs_2_, s32[3]{0:T(128)} %pad_add_fusion.refs_0_.refs_1_, s32[16]{0:T(128)} %refs_1_.10, f32[4,512,1024]{2,1,0:T(8,128)} %bitcast.35, f32[512,512]{1,0:T(8,128)} %get-tuple-element.55.refs_8_.refs_0_.refs_4_.refs_9_, f32[512,512]{1,0:T(8,128)} %copy-done.8, ...), custom_call_target="tpu_custom_call" | custom-call | flops 9663676416 | bytes 18874368 | tf_op jit(solution)/shard_map/pallas_call | solution.py:32
  156.9 0.9 collective-permute-done.15.refs_8_
  158.8 0.6 collective-permute-start.22
  159.5 1.5 collective-permute-start.23
  161.1 1.5 collective-permute-done.20.refs_6_
  162.6 1.5 collective-permute-done.21.refs_7_
  164.1 1.1 copy-done.19
  165.1 9.0 %shard_map.119.refs_4_ = f32[512,512]{1,0:T(8,128)} custom-call(s32[3]{0:T(128)} %pad_add_fusion.refs_0_.refs_1_, f32[4,512,1024]{2,1,0:T(8,128)} %bitcast.36, f32[512,512]{1,0:T(8,128)} %get-tuple-element.63.refs_0_.refs_2_, f32[512,512]{1,0:T(8,128)} %collective-permute-done.13.refs_3_, f32[512,512]{1,0:T(8,128)} %collective-permute-done.14.refs_4_, ...), custom_call_target="tpu_custom_call" | custom-call | flops 6442450944 | bytes 14680064 | tf_op jit(solution)/shard_map/pallas_call | solution.py:32
  174.1 4.8 %collective-permute-done.22.refs_10_ = f32[384,512]{1,0:T(8,128)} collective-permute-done((f32[384,512]{1,0:T(8,128)S(1)}, f32[384,512]{1,0:T(8,128)}, u32[]{:S(2)}, u32[]{:S(2)}) %collective-permute-start.22) | collective-permute-done | bytes 786464 | tf_op jit(solution)/shard_map/ppermute | solution.py:360
  179.3 12.8 %shard_map.120 = f32[8,512,128]{2,1,0:T(8,128)} custom-call(s32[3]{0:T(128)} %pad_add_fusion.refs_0_.refs_1_, s32[16]{0:T(128)} %refs_1_.10, s32[16]{0:T(128)} %refs_1_.11, s32[4]{0:T(128)} %refs_3_.7, f32[512,512]{1,0:T(8,128)} %shard_map.119.refs_4_, f32[4,128,512]{2,1,0:T(8,128)} %get-tuple-element.44.refs_6_.refs_5_, f32[4,128,512]{2,1,0:T(8,128)} %copy-done.13, ...), custom_call_target="tpu_custom_call" | custom-call | flops 3221225472 | bytes 9437184 | tf_op jit(solution)/shard_map/pallas_call | solution.py:32
  192.1 1.5 reduce-scatter.3.cloned.1.call-done
  193.6 1.0 slice_bitcast_fusion.2
  194.6 2.8 %collective-permute-start.17 = (f32[256,128]{1,0:T(8,128)S(1)}, f32[256,128]{1,0:T(8,128)S(1)}, u32[]{:S(2)}, u32[]{:S(2)}) collective-permute-start(f32[256,128]{1,0:T(8,128)S(1)} %get-tuple-element.73), channel_id=1, source_target_pairs={{0,0},{1,4},{2,8},{3,12},{4,1},{5,5},{6,9},{7,13},{8,2},{9,6},{10,... | collective-permute-start | bytes 393224 | tf_op jit(solution)/shard_map/ppermute | solution.py:525
  197.4 2.5 collective-permute-start.18
  199.9 33.4 %reduce-scatter.5.cloned.1.call-done = f32[1,512,128]{2,1,0:T(8,128)} async-done(((f32[8,512,128]{2,1,0:T(8,128)}), f32[1,512,128]{2,1,0:T(8,128)}) %reduce-scatter.5.cloned.1.call-update) | async-done | bytes 262160 | tf_op jit(solution)/shard_map/reduce_scatter | solution.py:513
  233.3 1.0 slice_bitcast_fusion
  234.3 1.9 collective-permute-start.24
  236.2 0.6 collective-permute-start.25
  236.8 0.6 copy-done.9
  237.5 2.1 shard_map.118
  239.6 8.2 %collective-permute-done.24.refs_4_ = f32[256,128]{1,0:T(8,128)S(1)} collective-permute-done((f32[256,128]{1,0:T(8,128)S(1)}, f32[256,128]{1,0:T(8,128)S(1)}, u32[]{:S(2)}, u32[]{:S(2)}) %collective-permute-start.24) | collective-permute-done | bytes 131104 | tf_op jit(solution)/shard_map/ppermute | solution.py:525
  247.8 0.7 copy-done.10
  248.5 2.1 shard_map.121
  (73 shorter events, 2.6 us)
Async XLA Ops:
  7.2 136.4 %all-gather.3.cloned.1.call-start = ((), (), s32[]{:S(2)}) async-start(), calls=%async_computation.4 | async-start | bytes 10485760 | tf_op jit(solution)/shard_map/all_gather | solution.py:413
  14.2 1.2 copy-start
  14.2 3.2 %copy-start.3 = (f32[128,512]{1,0:T(8,128)S(1)}, f32[128,512]{1,0:T(8,128)}, u32[]{:S(2)}) copy-start(f32[128,512]{1,0:T(8,128)} %get-tuple-element.35.refs_7_) | copy-start | bytes 786436
  14.3 179.4 %reduce-scatter.3.cloned.1.call-start = ((), (), s32[]{:S(2)}) async-start(), calls=%async_computation.2 | async-start | bytes 2359296 | tf_op jit(solution)/shard_map/reduce_scatter | solution.py:492
  15.5 39.6 %collective-permute-start.4 = (f32[512,512]{1,0:T(8,128)S(1)}, f32[512,512]{1,0:T(8,128)S(1)}, u32[]{:S(2)}, u32[]{:S(2)}) collective-permute-start(f32[512,512]{1,0:T(8,128)S(1)} %copy-done), channel_id=1, source_target_pairs={{0,2},{1,3},{2,0},{3,1},{4,6},{5,7},{6,4},{7,5},{8,10},{9,11},{10,... | collective-permute-start | bytes 3145736 | tf_op jit(solution)/shard_map/ppermute | solution.py:360
  15.5 41.0 %collective-permute-start.3 = (f32[512,512]{1,0:T(8,128)S(1)}, f32[512,512]{1,0:T(8,128)S(1)}, u32[]{:S(2)}, u32[]{:S(2)}) collective-permute-start(f32[512,512]{1,0:T(8,128)S(1)} %copy-done), channel_id=1, source_target_pairs={{0,1},{1,0},{2,3},{3,2},{4,5},{5,4},{6,7},{7,6},{8,9},{9,8},{10,11... | collective-permute-start | bytes 3145736 | tf_op jit(solution)/shard_map/ppermute | solution.py:360
  17.5 11.2 %collective-permute-start = (f32[128,512]{1,0:T(8,128)S(1)}, f32[128,512]{1,0:T(8,128)S(1)}, u32[]{:S(2)}, u32[]{:S(2)}) collective-permute-start(f32[128,512]{1,0:T(8,128)S(1)} %copy-done.3), channel_id=1, source_target_pairs={{0,8},{4,12},{8,16},{12,20},{16,24},{20,28},{24,0},{28,4},{1,9},{5... | collective-permute-start | bytes 786440 | tf_op jit(solution)/shard_map/ppermute | solution.py:339
  19.0 19.1 %collective-permute-start.1 = (f32[128,512]{1,0:T(8,128)S(1)}, f32[128,512]{1,0:T(8,128)S(1)}, u32[]{:S(2)}, u32[]{:S(2)}) collective-permute-start(f32[128,512]{1,0:T(8,128)S(1)} %copy-done.3), channel_id=1, source_target_pairs={{0,16},{4,20},{8,24},{12,28},{16,0},{20,4},{24,8},{28,12},{1,17},{... | collective-permute-start | bytes 786440 | tf_op jit(solution)/shard_map/ppermute | solution.py:339
  21.6 16.6 %collective-permute-start.2 = (f32[128,512]{1,0:T(8,128)S(1)}, f32[128,512]{1,0:T(8,128)S(1)}, u32[]{:S(2)}, u32[]{:S(2)}) collective-permute-start(f32[128,512]{1,0:T(8,128)S(1)} %copy-done.3), channel_id=1, source_target_pairs={{0,24},{4,28},{8,0},{12,4},{16,8},{20,12},{24,16},{28,20},{1,25},{... | collective-permute-start | bytes 786440 | tf_op jit(solution)/shard_map/ppermute | solution.py:339
  28.6 18.6 %copy-start.4 = (f32[128,512]{1,0:T(8,128)}, f32[128,512]{1,0:T(8,128)S(1)}, u32[]{:S(2)}) copy-start(f32[128,512]{1,0:T(8,128)S(1)} %collective-permute-done.refs_8_) | copy-start | bytes 786436
  38.2 9.1 %copy-start.5 = (f32[128,512]{1,0:T(8,128)}, f32[128,512]{1,0:T(8,128)S(1)}, u32[]{:S(2)}) copy-start(f32[128,512]{1,0:T(8,128)S(1)} %collective-permute-done.1.refs_9_) | copy-start | bytes 786436
  38.2 9.1 %copy-start.6 = (f32[128,512]{1,0:T(8,128)}, f32[128,512]{1,0:T(8,128)S(1)}, u32[]{:S(2)}) copy-start(f32[128,512]{1,0:T(8,128)S(1)} %collective-permute-done.2.refs_10_) | copy-start | bytes 786436
  38.2 32.6 %collective-permute-start.9 = (f32[512,512]{1,0:T(8,128)S(1)}, f32[512,512]{1,0:T(8,128)S(1)}, u32[]{:S(2)}, u32[]{:S(2)}) collective-permute-start(f32[512,512]{1,0:T(8,128)S(1)} %copy-done), channel_id=1, source_target_pairs={{16,8},{20,12},{0,24},{4,28},{17,9},{21,13},{1,25},{5,29},{18,10},... | collective-permute-start | bytes 3145736 | tf_op jit(solution)/shard_map/ppermute | solution.py:339
  50.7 20.1 %collective-permute-start.7 = (f32[4,128,512]{2,1,0:T(8,128)}, f32[4,128,512]{2,1,0:T(8,128)S(1)}, u32[]{:S(2)}, u32[]{:S(2)}) collective-permute-start(f32[4,128,512]{2,1,0:T(8,128)} %get-tuple-element.44.refs_6_.refs_5_), channel_id=1, source_target_pairs={{0,4},{4,0},{8,12},{12,8},{16,20},{20,16},{24,28},{28,24},{1,5},{5... | collective-permute-start | bytes 3145736 | tf_op jit(solution)/shard_map/ppermute | solution.py:353
  50.7 39.9 %collective-permute-start.8 = (f32[512,512]{1,0:T(8,128)S(1)}, f32[512,512]{1,0:T(8,128)S(1)}, u32[]{:S(2)}, u32[]{:S(2)}) collective-permute-start(f32[512,512]{1,0:T(8,128)S(1)} %copy-done), channel_id=1, source_target_pairs={{8,0},{12,4},{24,8},{28,12},{0,16},{4,20},{16,24},{20,28},{9,1},{1... | collective-permute-start | bytes 3145736 | tf_op jit(solution)/shard_map/ppermute | solution.py:339
  55.0 36.6 %copy-start.7 = (f32[512,512]{1,0:T(8,128)}, f32[512,512]{1,0:T(8,128)S(1)}, u32[]{:S(2)}) copy-start(f32[512,512]{1,0:T(8,128)S(1)} %collective-permute-done.4.refs_10_.refs_6_) | copy-start | bytes 3145732
  55.1 35.5 %collective-permute-start.5 = (f32[256,512]{1,0:T(8,128)S(1)}, f32[256,512]{1,0:T(8,128)S(1)}, u32[]{:S(2)}, u32[]{:S(2)}) collective-permute-start(f32[256,512]{1,0:T(8,128)S(1)} %slice.48), channel_id=1, source_target_pairs={{0,1},{1,0},{2,3},{3,2},{4,5},{5,4},{6,7},{7,6},{8,9},{9,8},{10,11... | collective-permute-start | bytes 1572872 | tf_op jit(solution)/shard_map/ppermute | solution.py:360
  56.4 35.2 %copy-start.8 = (f32[512,512]{1,0:T(8,128)}, f32[512,512]{1,0:T(8,128)S(1)}, u32[]{:S(2)}) copy-start(f32[512,512]{1,0:T(8,128)S(1)} %collective-permute-done.3.refs_9_.refs_5_) | copy-start | bytes 3145732
  56.5 34.1 %collective-permute-start.6 = (f32[256,512]{1,0:T(8,128)S(1)}, f32[256,512]{1,0:T(8,128)S(1)}, u32[]{:S(2)}, u32[]{:S(2)}) collective-permute-start(f32[256,512]{1,0:T(8,128)S(1)} %slice.49), channel_id=1, source_target_pairs={{0,2},{1,3},{2,0},{3,1},{4,6},{5,7},{6,4},{7,5},{8,10},{9,11},{10,... | collective-permute-start | bytes 1572872 | tf_op jit(solution)/shard_map/ppermute | solution.py:360
  70.8 30.1 %copy-start.14 = (f32[512,512]{1,0:T(8,128)}, f32[512,512]{1,0:T(8,128)S(1)}, u32[]{:S(2)}) copy-start(f32[512,512]{1,0:T(8,128)S(1)} %collective-permute-done.9.refs_11_) | copy-start | bytes 3145732
  70.8 30.0 %collective-permute-start.12 = (f32[512,512]{1,0:T(8,128)S(1)}, f32[512,512]{1,0:T(8,128)S(1)}, u32[]{:S(2)}, u32[]{:S(2)}) collective-permute-start(f32[512,512]{1,0:T(8,128)S(1)} %collective-permute-done.9.refs_11_), channel_id=1, source_target_pairs={{0,4},{4,0},{8,12},{12,8},{16,20},{20,16},{24,28},{28,24},{1,5},{5... | collective-permute-start | bytes 3145736 | tf_op jit(solution)/shard_map/ppermute | solution.py:353
  70.8 20.8 %copy-start.13 = (f32[4,128,512]{2,1,0:T(8,128)}, f32[4,128,512]{2,1,0:T(8,128)S(1)}, u32[]{:S(2)}) copy-start(f32[4,128,512]{2,1,0:T(8,128)S(1)} %collective-permute-done.7.refs_7_.refs_6_) | copy-start | bytes 3145732
  90.6 10.2 %copy-start.15 = (f32[512,512]{1,0:T(8,128)}, f32[512,512]{1,0:T(8,128)S(1)}, u32[]{:S(2)}) copy-start(f32[512,512]{1,0:T(8,128)S(1)} %collective-permute-done.8.refs_10_) | copy-start | bytes 3145732
  90.6 0.8 copy-start.20
  90.6 1.0 copy-start.21
  90.6 10.2 %collective-permute-start.10 = (f32[512,512]{1,0:T(8,128)S(1)}, f32[512,512]{1,0:T(8,128)}, u32[]{:S(2)}, u32[]{:S(2)}) collective-permute-start(f32[512,512]{1,0:T(8,128)S(1)} %copy-done), channel_id=1, source_target_pairs={{0,4},{4,0},{8,12},{12,8},{16,20},{20,16},{24,28},{28,24},{1,5},{5... | collective-permute-start | bytes 3145736 | tf_op jit(solution)/shard_map/ppermute | solution.py:353
  91.4 9.4 %collective-permute-start.11 = (f32[512,512]{1,0:T(8,128)S(1)}, f32[512,512]{1,0:T(8,128)}, u32[]{:S(2)}, u32[]{:S(2)}) collective-permute-start(f32[512,512]{1,0:T(8,128)S(1)} %collective-permute-done.8.refs_10_), channel_id=1, source_target_pairs={{0,4},{4,0},{8,12},{12,8},{16,20},{20,16},{24,28},{28,24},{1,5},{5... | collective-permute-start | bytes 3145736 | tf_op jit(solution)/shard_map/ppermute | solution.py:353
  100.8 1.1 copy-start.16
  101.9 55.9 %collective-permute-start.15 = (f32[768,512]{1,0:T(8,128)}, f32[768,512]{1,0:T(8,128)S(1)}, u32[]{:S(2)}, u32[]{:S(2)}) collective-permute-start(f32[768,512]{1,0:T(8,128)} %get-tuple-element.61.refs_7_), channel_id=1, source_target_pairs={{0,1},{1,0},{2,3},{3,2},{4,5},{5,4},{6,7},{7,6},{8,9},{9,8},{10,11... | collective-permute-start | bytes 4718600 | tf_op jit(solution)/shard_map/ppermute | solution.py:360
  102.4 55.4 %collective-permute-start.16 = (f32[768,512]{1,0:T(8,128)}, f32[768,512]{1,0:T(8,128)S(1)}, u32[]{:S(2)}, u32[]{:S(2)}) collective-permute-start(f32[768,512]{1,0:T(8,128)} %get-tuple-element.61.refs_7_), channel_id=1, source_target_pairs={{0,2},{1,3},{2,0},{3,1},{4,6},{5,7},{6,4},{7,5},{8,10},{9,11},{10,... | collective-permute-start | bytes 4718600 | tf_op jit(solution)/shard_map/ppermute | solution.py:360
  103.9 52.9 %collective-permute-start.13 = (f32[512,512]{1,0:T(8,128)}, f32[512,512]{1,0:T(8,128)}, u32[]{:S(2)}, u32[]{:S(2)}) collective-permute-start(f32[512,512]{1,0:T(8,128)} %get-tuple-element.63.refs_0_.refs_2_), channel_id=1, source_target_pairs={{8,0},{12,4},{24,8},{28,12},{0,16},{4,20},{16,24},{20,28},{9,1},{1... | collective-permute-start | bytes 3145736 | tf_op jit(solution)/shard_map/ppermute | solution.py:339
  107.4 49.5 %collective-permute-start.14 = (f32[512,512]{1,0:T(8,128)}, f32[512,512]{1,0:T(8,128)}, u32[]{:S(2)}, u32[]{:S(2)}) collective-permute-start(f32[512,512]{1,0:T(8,128)} %get-tuple-element.63.refs_0_.refs_2_), channel_id=1, source_target_pairs={{16,8},{20,12},{0,24},{4,28},{17,9},{21,13},{1,25},{5,29},{18,10},... | collective-permute-start | bytes 3145736 | tf_op jit(solution)/shard_map/ppermute | solution.py:339
  157.8 1.7 copy-start.1
  157.8 1.7 copy-start.2
  157.8 75.4 %reduce-scatter.5.cloned.1.call-start = ((), (), s32[]{:S(2)}) async-start(), calls=%async_computation.3 | async-start | bytes 2359296 | tf_op jit(solution)/shard_map/reduce_scatter | solution.py:513
  158.1 2.9 %collective-permute-start.19 = (f32[512,512]{1,0:T(8,128)}, f32[512,512]{1,0:T(8,128)S(1)}, u32[]{:S(2)}, u32[]{:S(2)}) collective-permute-start(f32[512,512]{1,0:T(8,128)} %get-tuple-element.63.refs_0_.refs_2_), channel_id=1, source_target_pairs={{0,4},{4,0},{8,12},{12,8},{16,20},{20,16},{24,28},{28,24},{1,5},{5... | collective-permute-start | bytes 3145736 | tf_op jit(solution)/shard_map/ppermute | solution.py:353
  158.2 4.4 %collective-permute-start.20 = (f32[512,512]{1,0:T(8,128)}, f32[512,512]{1,0:T(8,128)S(1)}, u32[]{:S(2)}, u32[]{:S(2)}) collective-permute-start(f32[512,512]{1,0:T(8,128)} %collective-permute-done.13.refs_3_), channel_id=1, source_target_pairs={{0,4},{4,0},{8,12},{12,8},{16,20},{20,16},{24,28},{28,24},{1,5},{5... | collective-permute-start | bytes 3145736 | tf_op jit(solution)/shard_map/ppermute | solution.py:353
  158.7 5.4 %collective-permute-start.21 = (f32[512,512]{1,0:T(8,128)}, f32[512,512]{1,0:T(8,128)S(1)}, u32[]{:S(2)}, u32[]{:S(2)}) collective-permute-start(f32[512,512]{1,0:T(8,128)} %collective-permute-done.14.refs_4_), channel_id=1, source_target_pairs={{0,4},{4,0},{8,12},{12,8},{16,20},{20,16},{24,28},{28,24},{1,5},{5... | collective-permute-start | bytes 3145736 | tf_op jit(solution)/shard_map/ppermute | solution.py:353
  158.8 20.1 %collective-permute-start.22 = (f32[384,512]{1,0:T(8,128)S(1)}, f32[384,512]{1,0:T(8,128)}, u32[]{:S(2)}, u32[]{:S(2)}) collective-permute-start(f32[384,512]{1,0:T(8,128)S(1)} %slice.42), channel_id=1, source_target_pairs={{0,1},{1,0},{2,3},{3,2},{4,5},{5,4},{6,7},{7,6},{8,9},{9,8},{10,11... | collective-permute-start | bytes 2359304 | tf_op jit(solution)/shard_map/ppermute | solution.py:360
  159.5 19.8 %collective-permute-start.23 = (f32[384,512]{1,0:T(8,128)S(1)}, f32[384,512]{1,0:T(8,128)}, u32[]{:S(2)}, u32[]{:S(2)}) collective-permute-start(f32[384,512]{1,0:T(8,128)S(1)} %slice.43), channel_id=1, source_target_pairs={{0,2},{1,3},{2,0},{3,1},{4,6},{5,7},{6,4},{7,5},{8,10},{9,11},{10,... | collective-permute-start | bytes 2359304 | tf_op jit(solution)/shard_map/ppermute | solution.py:360
  161.1 3.0 %copy-start.17 = (f32[512,512]{1,0:T(8,128)}, f32[512,512]{1,0:T(8,128)S(1)}, u32[]{:S(2)}) copy-start(f32[512,512]{1,0:T(8,128)S(1)} %collective-permute-done.19.refs_5_) | copy-start | bytes 3145732
  162.6 1.5 copy-start.18
  164.1 1.1 copy-start.19
  194.6 42.2 %collective-permute-start.17 = (f32[256,128]{1,0:T(8,128)S(1)}, f32[256,128]{1,0:T(8,128)S(1)}, u32[]{:S(2)}, u32[]{:S(2)}) collective-permute-start(f32[256,128]{1,0:T(8,128)S(1)} %get-tuple-element.73), channel_id=1, source_target_pairs={{0,0},{1,4},{2,8},{3,12},{4,1},{5,5},{6,9},{7,13},{8,2},{9,6},{10,... | collective-permute-start | bytes 393224 | tf_op jit(solution)/shard_map/ppermute | solution.py:525
  197.4 39.3 %collective-permute-start.18 = (f32[256,128]{1,0:T(8,128)S(1)}, f32[256,128]{1,0:T(8,128)S(1)}, u32[]{:S(2)}, u32[]{:S(2)}) collective-permute-start(f32[256,128]{1,0:T(8,128)S(1)} %get-tuple-element.72), channel_id=1, source_target_pairs={{0,16},{1,20},{2,24},{3,28},{4,17},{5,21},{6,25},{7,29},{8,18},{9,... | collective-permute-start | bytes 393224 | tf_op jit(solution)/shard_map/ppermute | solution.py:525
  234.3 13.5 %collective-permute-start.24 = (f32[256,128]{1,0:T(8,128)S(1)}, f32[256,128]{1,0:T(8,128)S(1)}, u32[]{:S(2)}, u32[]{:S(2)}) collective-permute-start(f32[256,128]{1,0:T(8,128)S(1)} %get-tuple-element.71), channel_id=1, source_target_pairs={{0,0},{1,4},{2,8},{3,12},{4,1},{5,5},{6,9},{7,13},{8,2},{9,6},{10,... | collective-permute-start | bytes 393224 | tf_op jit(solution)/shard_map/ppermute | solution.py:525
  236.2 11.6 %collective-permute-start.25 = (f32[256,128]{1,0:T(8,128)S(1)}, f32[256,128]{1,0:T(8,128)S(1)}, u32[]{:S(2)}, u32[]{:S(2)}) collective-permute-start(f32[256,128]{1,0:T(8,128)S(1)} %get-tuple-element.70), channel_id=1, source_target_pairs={{0,16},{1,20},{2,24},{3,28},{4,17},{5,21},{6,25},{7,29},{8,18},{9,... | collective-permute-start | bytes 393224 | tf_op jit(solution)/shard_map/ppermute | solution.py:525
  247.8 0.7 copy-start.12
  (3 other events, 2.0 us)
Sparse Core Ops, SparseCore 0:
  14.4 129.1 all-gather.2
  158.0 35.5 reduce-scatter.2
  195.9 37.3 reduce-scatter.4
